TPU v7x, 512 devices: a whole 4x8x8 slice. The times are simulated.
512 devices in a mesh: row: 32 (over x, z), col: 16 (over y, core).
Axes of the slice: x: 4, y: 8, z: 8, core: 2. Of those that a mesh axis runs over, the one named last changes fastest.
Arguments:
- saved_inputs: bfloat16 [1536, 8192], P('col', 'row'), may hold values from -6 to 6
- out_grad: bfloat16 [1536, 8192], P('col', 'row'), may hold values from -0.59765625 to 0.59765625
- gate_pre: bfloat16 [1536, 14336], P('row', 'col'), may hold values from -8 to 8
- up_pre: bfloat16 [1536, 14336], P('row', 'col'), may hold values from -6 to 6
- gate_weight: bfloat16 [8192, 14336], P('row', 'col'), may hold values from -0.0625 to 0.0625
- up_weight: bfloat16 [8192, 14336], P('row', 'col'), may hold values from -0.0625 to 0.0625
- down_weight: bfloat16 [14336, 8192], P('col', 'row'), may hold values from -0.046875 to 0.046875
Outputs:
- input_grad: bfloat16 [1536, 8192], P('col', 'row')
- gate_grad: bfloat16 [8192, 14336], P('row', 'col')
- up_grad: bfloat16 [8192, 14336], P('row', 'col')
- down_grad: bfloat16 [14336, 8192], P('col', 'row')
All inputs are finite; a program needn't handle non-finite values.
Results may differ from a plain program's by a relative error of at most 0.033.
Values may be sent and summed in bfloat16 or wider, within the bound.
No kernel may reach another device: no remote copies, remote signals or barrier semaphores. Data moves between devices by JAX's collectives and lax.ppermute only.
A program may use at most 64 MiB of HBM per device.

v0:
```python
import jax
import jax.numpy as jnp
from jax import lax
from jax.sharding import PartitionSpec as P


def derivatives(hidden_grad, gate_pre, up_pre):
    gate_val = gate_pre.astype(jnp.float32)
    up_val = up_pre.astype(jnp.float32)
    sigma = jax.nn.sigmoid(gate_val)
    silu = gate_val * sigma
    gate_delta = (hidden_grad * up_val * sigma * (1.0 + gate_val * (1.0 - sigma))).astype(
        jnp.bfloat16
    )
    up_delta = (hidden_grad * silu).astype(jnp.bfloat16)
    hidden = (silu * up_val).astype(jnp.bfloat16)
    return (gate_delta, up_delta, hidden)


def contract_rows(left, right):
    return lax.dot_general(
        left, right, (((0,), (0,)), ((), ())), preferred_element_type=jnp.float32
    )


def contract_cols(left, right):
    return lax.dot_general(
        left, right, (((1,), (1,)), ((), ())), preferred_element_type=jnp.float32
    )


def body(saved_inputs, out_grad, gate_pre, up_pre, gate_weight, up_weight, down_weight):
    inputs_all, grads_all = (
        lax.all_gather(saved_inputs, "col", axis=0, tiled=True),
        lax.all_gather(out_grad, "col", axis=0, tiled=True),
    )
    hidden_local = lax.psum_scatter(
        contract_cols(grads_all, down_weight).astype(jnp.bfloat16),
        "row",
        scatter_dimension=0,
        tiled=True,
    ).astype(jnp.float32)
    gate_local, up_local, hidden_part = derivatives(hidden_local, gate_pre, up_pre)
    gate_delta, up_delta, hidden = (
        lax.all_gather(gate_local, "row", axis=0, tiled=True),
        lax.all_gather(up_local, "row", axis=0, tiled=True),
        lax.all_gather(hidden_part, "row", axis=0, tiled=True),
    )
    down_grad = contract_rows(hidden, grads_all).astype(jnp.bfloat16)
    gate_grad = contract_rows(inputs_all, gate_delta).astype(jnp.bfloat16)
    up_grad = contract_rows(inputs_all, up_delta).astype(jnp.bfloat16)
    input_grad = lax.psum_scatter(
        (contract_cols(gate_delta, gate_weight) + contract_cols(up_delta, up_weight)).astype(
            jnp.bfloat16
        ),
        "col",
        scatter_dimension=0,
        tiled=True,
    )
    return (input_grad, gate_grad, up_grad, down_grad)


def solution(mesh):
    return jax.shard_map(
        body,
        mesh=mesh,
        in_specs=(
            P("col", "row"),
            P("col", "row"),
            P("row", "col"),
            P("row", "col"),
            P("row", "col"),
            P("row", "col"),
            P("col", "row"),
        ),
        out_specs=(P("col", "row"), P("row", "col"), P("row", "col"), P("col", "row")),
        check_vma=False,
    )
```

profile of v0, /device:TPU:29, one launch (start us, length us, event | category | flops | bytes accessed | tf_op | source)
XLA Modules:
  0.0 570.0 jit_solution(18175896152742828323)
XLA Ops:
  7.2 0.0 reduce-scatter.3.cloned.1.call-start
  7.2 18.7 %all_gather.15 = bf16[1536,256]{1,0:T(8,128)(2,1)S(1)} all-gather(bf16[96,256]{1,0:T(8,128)(2,1)} %param.8), channel_id=1, replica_groups=mesh['row'=32,'col'=16] {'col'}, dimensions={0}, use_global_device_ids=true | all-gather | bytes 835584 | tf_op jit(solution)/shard_map/all_gather | solution.py:35
  25.9 1.0 copy-done.2
  26.9 2.6 convolution_convert_fusion
  29.5 0.0 all-gather.4.cloned.1.call-start
  29.5 209.5 %reduce-scatter.3.cloned.1.call-done = bf16[48,896]{1,0:T(8,128)(2,1)} async-done(((bf16[1536,896]{1,0:T(8,128)(2,1)}), bf16[48,896]{1,0:T(8,128)(2,1)}) %reduce-scatter.3.cloned.1.call-update) | async-done | bytes 86032 | tf_op jit(solution)/shard_map/reduce_scatter | solution.py:37
  239.1 1.7 fusion.7
  240.8 0.0 all-gather.6.cloned.1.call-start
  240.8 0.7 all-gather.6.cloned.1.call-update
  241.6 0.5 all-gather.8.cloned.1.call-update
  242.1 0.0 reduce-scatter.5.cloned.1.call-start
  242.2 85.4 %all-gather.4.cloned.1.call-done = bf16[1536,896]{1,0:T(8,128)(2,1)} async-done(((bf16[48,896]{1,0:T(8,128)(2,1)}), bf16[1536,896]{1,0:T(8,128)(2,1)}) %all-gather.4.cloned.1.call-update) | async-done | bytes 2752528 | tf_op jit(solution)/shard_map/all_gather | solution.py:45
  327.6 2.8 fusion.12
  330.4 83.2 %all-gather.6.cloned.1.call-done = bf16[1536,896]{1,0:T(8,128)(2,1)} async-done(((bf16[48,896]{1,0:T(8,128)(2,1)}), bf16[1536,896]{1,0:T(8,128)(2,1)}) %all-gather.6.cloned.1.call-update) | async-done | bytes 2752528 | tf_op jit(solution)/shard_map/all_gather | solution.py:46
  413.6 3.7 fusion
  417.3 21.9 %all_gather.18 = bf16[1536,256]{1,0:T(8,128)(2,1)S(1)} all-gather(bf16[96,256]{1,0:T(8,128)(2,1)S(1)} %copy-done.8), channel_id=1, replica_groups=mesh['row'=32,'col'=16] {'col'}, dimensions={0}, use_global_device_ids=true | all-gather | bytes 835584 | tf_op jit(solution)/shard_map/all_gather | solution.py:34
  439.3 0.9 copy-done.3
  440.2 3.6 fusion.1
  443.8 2.0 copy.11
  445.8 2.8 fusion.2
  448.6 2.0 copy.12
  450.6 48.3 %all-gather.8.cloned.1.call-done = bf16[1536,896]{1,0:T(8,128)(2,1)} async-done(((bf16[48,896]{1,0:T(8,128)(2,1)}), bf16[1536,896]{1,0:T(8,128)(2,1)}) %all-gather.8.cloned.1.call-update) | async-done | bytes 2752528 | tf_op jit(solution)/shard_map/all_gather | solution.py:47
  498.9 3.7 convolution_convert_fusion.1
  502.6 60.9 %reduce-scatter.5.cloned.1.call-done = bf16[96,256]{1,0:T(8,128)(2,1)} async-done(((bf16[1536,256]{1,0:T(8,128)(2,1)}), bf16[96,256]{1,0:T(8,128)(2,1)}) %reduce-scatter.5.cloned.1.call-update) | async-done | bytes 49168 | tf_op jit(solution)/shard_map/reduce_scatter | solution.py:52
  (20 shorter events, 0.1 us)
Async XLA Ops:
  7.2 19.7 %copy-start = (bf16[896,256]{1,0:T(8,128)(2,1)S(1)}, bf16[896,256]{1,0:T(8,128)(2,1)}, u32[]{:S(2)}) copy-start(bf16[896,256]{1,0:T(8,128)(2,1)} %param.13) | copy-start | bytes 1376260
  7.2 231.9 %reduce-scatter.3.cloned.1.call-start = ((), (), s32[]{:S(2)}) async-start(), calls=%async_computation.2 | async-start | bytes 2838528 | tf_op jit(solution)/shard_map/reduce_scatter | solution.py:37
  25.9 1.0 copy-start.2
  26.9 212.2 %copy-start.6 = (bf16[48,896]{1,0:T(8,128)(2,1)S(1)}, bf16[48,896]{1,0:T(8,128)(2,1)}, u32[]{:S(2)}) copy-start(bf16[48,896]{1,0:T(8,128)(2,1)} %param.10) | copy-start | bytes 258052
  26.9 212.2 %copy-start.7 = (bf16[48,896]{1,0:T(8,128)(2,1)S(1)}, bf16[48,896]{1,0:T(8,128)(2,1)}, u32[]{:S(2)}) copy-start(bf16[48,896]{1,0:T(8,128)(2,1)} %param.9) | copy-start | bytes 258052
  29.5 298.1 %copy-start.5 = (bf16[256,896]{1,0:T(8,128)(2,1)S(1)}, bf16[256,896]{1,0:T(8,128)(2,1)}, u32[]{:S(2)}) copy-start(bf16[256,896]{1,0:T(8,128)(2,1)} %param.11) | copy-start | bytes 1376260
  29.5 298.1 %all-gather.4.cloned.1.call-start = ((), (), s32[]{:S(2)}) async-start(), calls=%async_computation.3 | async-start | bytes 2838528 | tf_op jit(solution)/shard_map/all_gather | solution.py:45
  240.8 172.8 %all-gather.6.cloned.1.call-start = ((), (), s32[]{:S(2)}) async-start(), calls=%async_computation.4 | async-start | bytes 2838528 | tf_op jit(solution)/shard_map/all_gather | solution.py:46
  241.5 257.4 %all-gather.8.cloned.1.call-start = ((), (), s32[]{:S(2)}) async-start(), calls=%async_computation.6 | async-start | bytes 2838528 | tf_op jit(solution)/shard_map/all_gather | solution.py:47
  242.1 171.5 %copy-start.4 = (bf16[256,896]{1,0:T(8,128)(2,1)S(1)}, bf16[256,896]{1,0:T(8,128)(2,1)}, u32[]{:S(2)}) copy-start(bf16[256,896]{1,0:T(8,128)(2,1)} %param.12) | copy-start | bytes 1376260
  242.1 321.3 %reduce-scatter.5.cloned.1.call-start = ((), (), s32[]{:S(2)}) async-start(), calls=%async_computation.5 | async-start | bytes 835584 | tf_op jit(solution)/shard_map/reduce_scatter | solution.py:52
  330.4 86.9 %copy-start.8 = (bf16[96,256]{1,0:T(8,128)(2,1)S(1)}, bf16[96,256]{1,0:T(8,128)(2,1)}, u32[]{:S(2)}) copy-start(bf16[96,256]{1,0:T(8,128)(2,1)} %param.7) | copy-start | bytes 147460
  439.3 0.9 copy-start.3
  440.2 5.6 copy-start.1
Sparse Core Ops, SparseCore 0:
  29.6 209.4 reduce-scatter.2
  243.3 84.2 all-gather.3
  331.8 81.7 all-gather.5
  417.1 81.7 all-gather.7
  502.4 61.0 reduce-scatter.4
where the time goes:
time: 570 us
  waiting for transfers between devices  489 us (86%)
  blocking collectives  40.6 us (7%)
  matrix products  19.1 us (3%)
  between operations  13.8 us (2%)
  local copies, waits for them, and re-layouts  5.87 us (1%)
    reduce_scatter x1, waiting for transfers between devices, body(): lax.psum_scatter(contract_cols(grads_all, down_weight).astype(jnp.bfloat1...  210 us
    all_gather x1, waiting for transfers between devices, body(): lax.all_gather(gate_local, 'row', axis=0, tiled=True)  85.4 us
    all_gather x1, waiting for transfers between devices, body(): lax.all_gather(up_local, 'row', axis=0, tiled=True)  83.2 us
    reduce_scatter x1, waiting for transfers between devices, body(): lax.psum_scatter((contract_cols(gate_delta, gate_weight) + contract_cols(...  60.9 us
    all_gather x1, waiting for transfers between devices, body(): lax.all_gather(hidden_part, 'row', axis=0, tiled=True)  48.3 us
    all_gather x1, blocking collectives, body(): lax.all_gather(saved_inputs, 'col', axis=0, tiled=True)  21.9 us
    all_gather x1, blocking collectives, body(): lax.all_gather(out_grad, 'col', axis=0, tiled=True)  18.7 us
  transfers between devices with their start and end apart: 5, of which 5 were waited for; matrix products, arithmetic and copies ran while one was open for 4% of the time, Pallas kernels for 0%

commit v1 on v0

v1 whole, which is shorter than its diff:
```python
import jax
import jax.numpy as jnp
from jax import lax
from jax.sharding import Mesh, PartitionSpec as P

BF = jnp.bfloat16
F32 = jnp.float32
SWAP = [(0, 1), (1, 0)]


def contract_rows(left, right):
    return lax.dot_general(left, right, (((0,), (0,)), ((), ())), preferred_element_type=F32)


def contract_cols(left, right):
    return lax.dot_general(left, right, (((1,), (1,)), ((), ())), preferred_element_type=F32)


def swap(value):
    return lax.ppermute(value, "zw", SWAP)


def halves(value, w):
    n = value.shape[0] // 2
    return (
        lax.dynamic_slice_in_dim(value, w * n, n, 0),
        lax.dynamic_slice_in_dim(value, (1 - w) * n, n, 0),
    )


def gather_tokens(value, w):
    mine, theirs = halves(value, w)
    both = jnp.concatenate([mine, swap(theirs)], axis=1)
    return lax.all_gather(both, ("y", "core"), axis=0, tiled=True)


def scatter_sum(value, axis, parts):
    arrived = lax.all_to_all(value, axis, 0, 0, tiled=True)
    return arrived.astype(F32).sum(axis=0)


def weight_grad(partial, n, axis):
    own = lax.slice_in_dim(partial, 0, n, axis=axis)
    other = lax.slice_in_dim(partial, n, 2 * n, axis=axis)
    return (own + swap(other.astype(BF)).astype(F32)).astype(BF)


def body(saved_inputs, out_grad, gate_pre, up_pre, gate_weight, up_weight, down_weight):
    w = lax.axis_index("zw")
    width = out_grad.shape[1]
    tokens = gate_pre.shape[0]
    units = gate_pre.shape[1]
    down_w = jnp.concatenate([down_weight, swap(down_weight)], axis=1)
    grads = gather_tokens(out_grad, w)
    pre = lax.all_gather(
        jnp.concatenate([gate_pre, up_pre], axis=1), ("x", "zq"), axis=0, tiled=True
    )
    gate_w = jnp.concatenate([gate_weight, swap(gate_weight)], axis=0)
    up_w = jnp.concatenate([up_weight, swap(up_weight)], axis=0)

    part = contract_cols(grads, down_w).astype(BF)
    part = scatter_sum(part.reshape(4, 4 * tokens, units), "x", 4).astype(BF)
    part = scatter_sum(part.reshape(4, tokens, units), "zq", 4).astype(BF)
    hidden_grad = lax.all_to_all(
        jnp.broadcast_to(part[None], (4,) + part.shape), "zq", 0, 0, tiled=True
    ).reshape(4 * tokens, units)
    hidden_grad = lax.all_to_all(
        jnp.broadcast_to(hidden_grad[None], (4,) + hidden_grad.shape), "x", 0, 0, tiled=True
    ).reshape(16 * tokens, units)

    inputs = gather_tokens(saved_inputs, w)
    gate_val = pre[:, :units].astype(F32)
    up_val = pre[:, units:].astype(F32)
    sigma = jax.nn.sigmoid(gate_val)
    silu = gate_val * sigma
    hidden = (silu * up_val).astype(BF)
    hidden_grad = hidden_grad.astype(F32)
    gate_delta = (hidden_grad * up_val * sigma * (1.0 + gate_val * (1.0 - sigma))).astype(BF)
    up_delta = (hidden_grad * silu).astype(BF)

    down_grad = weight_grad(contract_rows(hidden, grads), width, 1)
    term = (contract_cols(gate_delta, gate_w) + contract_cols(up_delta, up_w)).astype(BF)
    term = lax.all_to_all(term.reshape(8, 2, tokens, 2 * width), "core", 1, 1, tiled=True)
    term = term.astype(F32).sum(axis=1).astype(BF)
    term = scatter_sum(term, "y", 8).astype(BF)
    gate_grad = weight_grad(contract_rows(inputs, gate_delta), width, 0)
    up_grad = weight_grad(contract_rows(inputs, up_delta), width, 0)

    mine, theirs = term[:, :width], swap(term[:, width:])
    input_grad = jnp.where(
        w == 0,
        jnp.concatenate([mine, theirs], axis=0),
        jnp.concatenate([theirs, mine], axis=0),
    )
    return (input_grad, gate_grad, up_grad, down_grad)


def solution(mesh):
    fine = Mesh(mesh.devices.reshape(4, 4, 2, 8, 2), ("x", "zq", "zw", "y", "core"))
    row, col = ("x", "zq", "zw"), ("y", "core")
    return jax.shard_map(
        body,
        mesh=fine,
        in_specs=(
            P(col, row),
            P(col, row),
            P(row, col),
            P(row, col),
            P(row, col),
            P(row, col),
            P(col, row),
        ),
        out_specs=(P(col, row), P(row, col), P(row, col), P(col, row)),
        check_vma=False,
    )
```

time: 570 us -> 208 us (0.36)
  the two profiles are of different devices: /device:TPU:29 before, /device:TPU:10 now
where the time goes in v1:
time: 208 us; the launch traced here: 207 us
  blocking collectives  111 us (53%)
  starting transfers between devices  38.4 us (18%)
  waiting for transfers between devices  16.5 us (8%)
  between operations  14.3 us (7%)
  matrix products  10.9 us (5%)
  other arithmetic  10.8 us (5%)
  local copies, waits for them, and re-layouts  4.69 us (2%)
    all_to_all x2, blocking collectives, scatter_sum(): arrived = lax.all_to_all(value, axis, 0, 0, tiled=True)  55 us
    all_gather x2, blocking collectives, gather_tokens(): return lax.all_gather(both, ('y', 'core'), axis=0, tiled=True)  36.8 us
    ppermute x9, starting transfers between devices, swap(): return lax.ppermute(value, 'zw', SWAP)  27.5 us
    ppermute x9, waiting for transfers between devices, swap(): return lax.ppermute(value, 'zw', SWAP)  16.5 us
    all_to_all x1, blocking collectives, body(): lax.all_to_all(jnp.broadcast_to(part[None], (4,) + part.shape), 'zq', 0,...  14.8 us
    all_to_all x1, starting transfers between devices, scatter_sum(): arrived = lax.all_to_all(value, axis, 0, 0, tiled=True)  5.6 us
    dot_general x3, matrix products, contract_rows(): lax.dot_general(left, right, (((0,), (0,)), ((), ())), preferred_element_...  5.53 us
    dot_general x3, matrix products, contract_cols(): lax.dot_general(left, right, (((1,), (1,)), ((), ())), preferred_element_...  5.35 us
  transfers between devices with their start and end apart: 12, of which 3 were waited for; matrix products, arithmetic and copies ran while one was open for 11% of the time, Pallas kernels for 0%

profile of v1, /device:TPU:10, one launch (start us, length us, event | category | flops | bytes accessed | tf_op | source)
XLA Modules:
  0.0 206.6 jit_solution(13510298235011680839)
XLA Ops:
  9.6 4.3 %collective-permute-start = (bf16[48,256]{1,0:T(8,128)(2,1)S(1)}, bf16[48,256]{1,0:T(8,128)(2,1)S(1)}, u32[]{:S(2)}, u32[]{:S(2)}) collective-permute-start(bf16[48,256]{1,0:T(8,128)(2,1)S(1)} %get-tuple-element.11), channel_id=1, source_target_pairs={{0,16},{16,0},{1,17},{17,1},{2,18},{18,2},{3,19},{19,3},{4,20},{20... | collective-permute-start | bytes 73736 | tf_op jit(solution)/shard_map/ppermute | solution.py:20
  15.9 18.3 %all_gather.9 = bf16[768,512]{1,0:T(8,128)(2,1)S(1)} all-gather(bf16[48,512]{1,0:T(8,128)(2,1)S(1)} %pad_maximum_fusion.1), channel_id=1, replica_groups=mesh['x'=4,'zq'=4,'zw'=2,'y'=8,'core'=2] {'y','core'}, dimensions={0}, use_global_device_ids=true | all-gather | bytes 835584 | tf_op jit(solution)/shard_map/all_gather | solution.py:34
  34.2 2.3 %convolution_convert_fusion = bf16[768,896]{1,0:T(8,128)(2,1)S(1)} fusion(bf16[768,512]{1,0:T(8,128)(2,1)S(1)} %all_gather.9, bf16[896,256]{1,0:T(8,128)(2,1)S(1)} %collective-permute-done.1, bf16[896,256]{1,0:T(8,128)(2,1)} %param.13), kind=kOutput, calls=%fused_computation.15 | convolution fusion | flops 707166208 | bytes 3080192 | tf_op jit(solution)/shard_map/dot_general | solution.py:16
  36.5 24.8 %all_to_all.30 = bf16[4,192,896]{2,1,0:T(8,128)(2,1)S(1)} all-to-all(bf16[4,192,896]{2,1,0:T(8,128)(2,1)S(1)} %bitcast.16), channel_id=1, replica_groups=mesh['x'=4,'zq'=4,'zw'=2,'y'=8,'core'=2] {'x'}, dimensions={0} | all-to-all | bytes 2752512 | tf_op jit(solution)/shard_map/all_to_all | solution.py:38
  61.7 30.1 %all_to_all.31 = bf16[4,48,896]{2,1,0:T(8,128)(2,1)S(1)} all-to-all(bf16[4,48,896]{2,1,0:T(8,128)(2,1)S(1)} %bitcast.17), channel_id=1, replica_groups=mesh['x'=4,'zq'=4,'zw'=2,'y'=8,'core'=2] {'zq'}, dimensions={0} | all-to-all | bytes 688128 | tf_op jit(solution)/shard_map/all_to_all | solution.py:38
  91.9 14.8 %all_to_all.32 = bf16[4,48,896]{2,1,0:T(8,128)(2,1)S(1)} all-to-all(bf16[4,48,896]{2,1,0:T(8,128)(2,1)S(1)} %broadcast_in_dim.6), channel_id=1, replica_groups=mesh['x'=4,'zq'=4,'zw'=2,'y'=8,'core'=2] {'zq'}, dimensions={0} | all-to-all | bytes 688128 | tf_op jit(solution)/shard_map/all_to_all | solution.py:64
  107.9 5.3 %all-to-all-start.3 = ((bf16[4,192,896]{2,1,0:T(8,128)(2,1)}), bf16[4,192,896]{2,1,0:T(8,128)(2,1)S(1)}, u32[]{:S(2)}, u32[]{:S(2)}) async-start(bf16[4,192,896]{2,1,0:T(8,128)(2,1)} %broadcast_in_dim.15), calls=%async_computation.3 | async-start | bytes 2752512 | tf_op jit(solution)/shard_map/all_to_all | solution.py:67
  113.2 2.4 %collective-permute-start.5 = (bf16[48,256]{1,0:T(8,128)(2,1)S(1)}, bf16[48,256]{1,0:T(8,128)(2,1)S(1)}, u32[]{:S(2)}, u32[]{:S(2)}) collective-permute-start(bf16[48,256]{1,0:T(8,128)(2,1)S(1)} %get-tuple-element.7), channel_id=1, source_target_pairs={{0,16},{16,0},{1,17},{17,1},{2,18},{18,2},{3,19},{19,3},{4,20},{20... | collective-permute-start | bytes 73736 | tf_op jit(solution)/shard_map/ppermute | solution.py:20
  115.6 3.5 %collective-permute-start.3 = (bf16[256,896]{1,0:T(8,128)(2,1)S(1)}, bf16[256,896]{1,0:T(8,128)(2,1)}, u32[]{:S(2)}, u32[]{:S(2)}) collective-permute-start(bf16[256,896]{1,0:T(8,128)(2,1)S(1)} %copy-done.7), channel_id=1, source_target_pairs={{0,16},{16,0},{1,17},{17,1},{2,18},{18,2},{3,19},{19,3},{4,20},{20... | collective-permute-start | bytes 1376264 | tf_op jit(solution)/shard_map/ppermute | solution.py:20
  119.1 2.4 %collective-permute-start.2 = (bf16[256,896]{1,0:T(8,128)(2,1)S(1)}, bf16[256,896]{1,0:T(8,128)(2,1)S(1)}, u32[]{:S(2)}, u32[]{:S(2)}) collective-permute-start(bf16[256,896]{1,0:T(8,128)(2,1)S(1)} %copy-done.8), channel_id=1, source_target_pairs={{0,16},{16,0},{1,17},{17,1},{2,18},{18,2},{3,19},{19,3},{4,20},{20... | collective-permute-start | bytes 1376264 | tf_op jit(solution)/shard_map/ppermute | solution.py:20
  121.5 18.5 %all_gather.11 = bf16[768,512]{1,0:T(8,128)(2,1)S(1)} all-gather(bf16[48,512]{1,0:T(8,128)(2,1)S(1)} %pad_maximum_fusion.2), channel_id=1, replica_groups=mesh['x'=4,'zq'=4,'zw'=2,'y'=8,'core'=2] {'y','core'}, dimensions={0}, use_global_device_ids=true | all-gather | bytes 835584 | tf_op jit(solution)/shard_map/all_gather | solution.py:34
  140.0 3.3 %fusion.3 = (bf16[768,896]{1,0:T(8,128)(2,1)S(1)}, bf16[768,896]{1,0:T(8,128)(2,1)S(1)}) fusion(bf16[4,192,896]{2,1,0:T(8,128)(2,1)S(1)} %all-to-all-done.3, bf16[768,1792]{1,0:T(8,128)(2,1)} %all-gather.2.cloned.1.call-done), kind=kLoop, calls=%fused_computation.9 | loop fusion | flops 11010048 | bytes 6881280 | tf_op jit(solution)/shard_map/convert_element_type | solution.py:78
  143.4 2.3 %fusion.31 = f32[512,896]{1,0:T(8,128)} fusion(bf16[768,512]{1,0:T(8,128)(2,1)S(1)} %all_gather.11, bf16[768,896]{1,0:T(8,128)(2,1)S(1)} %get-tuple-element.5), kind=kOutput, calls=%fused_computation.52 | convolution fusion | flops 704643072 | bytes 3997696 | tf_op jit(solution)/shard_map/dot_general | solution.py:12
  147.6 2.3 %fusion.30 = f32[512,896]{1,0:T(8,128)} fusion(bf16[768,512]{1,0:T(8,128)(2,1)S(1)} %all_gather.11, bf16[768,896]{1,0:T(8,128)(2,1)S(1)} %get-tuple-element.4), kind=kOutput, calls=%fused_computation.51 | convolution fusion | flops 704643072 | bytes 3997696 | tf_op jit(solution)/shard_map/dot_general | solution.py:12
  151.0 4.4 %all_to_all.33 = bf16[8,2,48,512]{3,2,0,1:T(8,128)(2,1)S(1)} all-to-all(bf16[8,2,48,512]{3,2,0,1:T(8,128)(2,1)S(1)} %copy.12), channel_id=1, replica_groups=mesh['x'=4,'zq'=4,'zw'=2,'y'=8,'core'=2] {'core'}, dimensions={1} | all-to-all | bytes 1572864 | tf_op jit(solution)/shard_map/all_to_all | solution.py:83
  156.4 5.6 %all-to-all-start.5 = ((bf16[8,48,512]{2,1,0:T(8,128)(2,1)}), bf16[8,48,512]{2,1,0:T(8,128)(2,1)S(1)}, u32[]{:S(2)}, u32[]{:S(2)}) async-start(bf16[8,48,512]{2,1,0:T(8,128)(2,1)} %reduce_sum.50), calls=%async_computation.5 | async-start | bytes 786432 | tf_op jit(solution)/shard_map/all_to_all | solution.py:38
  163.3 3.4 %collective-permute-start.6 = (bf16[256,896]{1,0:T(8,128)(2,1)S(1)}, bf16[256,896]{1,0:T(8,128)(2,1)S(1)}, u32[]{:S(2)}, u32[]{:S(2)}) collective-permute-start(bf16[256,896]{1,0:T(8,128)(2,1)S(1)} %slice.79), channel_id=1, source_target_pairs={{0,16},{16,0},{1,17},{17,1},{2,18},{18,2},{3,19},{19,3},{4,20},{20... | collective-permute-start | bytes 1376264 | tf_op jit(solution)/shard_map/ppermute | solution.py:20
  168.0 2.5 %collective-permute-start.7 = (bf16[256,896]{1,0:T(8,128)(2,1)S(1)}, bf16[256,896]{1,0:T(8,128)(2,1)S(1)}, u32[]{:S(2)}, u32[]{:S(2)}) collective-permute-start(bf16[256,896]{1,0:T(8,128)(2,1)S(1)} %slice.78), channel_id=1, source_target_pairs={{0,16},{16,0},{1,17},{17,1},{2,18},{18,2},{3,19},{19,3},{4,20},{20... | collective-permute-start | bytes 1376264 | tf_op jit(solution)/shard_map/ppermute | solution.py:20
  171.6 3.7 %collective-permute-start.8 = (bf16[896,256]{1,0:T(8,128)(2,1)S(1)}, bf16[896,256]{1,0:T(8,128)(2,1)S(1)}, u32[]{:S(2)}, u32[]{:S(2)}) collective-permute-start(bf16[896,256]{1,0:T(8,128)(2,1)S(1)} %slice.77), channel_id=1, source_target_pairs={{0,16},{16,0},{1,17},{17,1},{2,18},{18,2},{3,19},{19,3},{4,20},{20... | collective-permute-start | bytes 1376264 | tf_op jit(solution)/shard_map/ppermute | solution.py:20
  175.3 3.3 %collective-permute-done.6 = bf16[256,896]{1,0:T(8,128)(2,1)S(1)} collective-permute-done((bf16[256,896]{1,0:T(8,128)(2,1)S(1)}, bf16[256,896]{1,0:T(8,128)(2,1)S(1)}, u32[]{:S(2)}, u32[]{:S(2)}) %collective-permute-start.6) | collective-permute-done | bytes 458784 | tf_op jit(solution)/shard_map/ppermute | solution.py:20
  179.5 9.0 %collective-permute-done.7 = bf16[256,896]{1,0:T(8,128)(2,1)S(1)} collective-permute-done((bf16[256,896]{1,0:T(8,128)(2,1)S(1)}, bf16[256,896]{1,0:T(8,128)(2,1)S(1)}, u32[]{:S(2)}, u32[]{:S(2)}) %collective-permute-start.7) | collective-permute-done | bytes 458784 | tf_op jit(solution)/shard_map/ppermute | solution.py:20
  189.4 3.4 %collective-permute-start.4 = (bf16[48,256]{1,0:T(8,128)(2,1)S(1)}, bf16[48,256]{1,0:T(8,128)(2,1)S(1)}, u32[]{:S(2)}, u32[]{:S(2)}) collective-permute-start(bf16[48,256]{1,0:T(8,128)(2,1)S(1)} %get-tuple-element.9), channel_id=1, source_target_pairs={{0,16},{16,0},{1,17},{17,1},{2,18},{18,2},{3,19},{19,3},{4,20},{20... | collective-permute-start | bytes 73736 | tf_op jit(solution)/shard_map/ppermute | solution.py:20
  192.8 4.2 %collective-permute-done.8 = bf16[896,256]{1,0:T(8,128)(2,1)S(1)} collective-permute-done((bf16[896,256]{1,0:T(8,128)(2,1)S(1)}, bf16[896,256]{1,0:T(8,128)(2,1)S(1)}, u32[]{:S(2)}, u32[]{:S(2)}) %collective-permute-start.8) | collective-permute-done | bytes 458784 | tf_op jit(solution)/shard_map/ppermute | solution.py:20
  197.1 2.0 fusion.12
  (52 shorter events, 16.1 us)
Async XLA Ops:
  7.2 132.8 %all-gather.2.cloned.1.call-start = ((), (), s32[]{:S(2)}) async-start(), calls=%async_computation.6 | async-start | bytes 2924544 | tf_op jit(solution)/shard_map/all_gather | solution.py:55
  9.6 6.2 %collective-permute-start = (bf16[48,256]{1,0:T(8,128)(2,1)S(1)}, bf16[48,256]{1,0:T(8,128)(2,1)S(1)}, u32[]{:S(2)}, u32[]{:S(2)}) collective-permute-start(bf16[48,256]{1,0:T(8,128)(2,1)S(1)} %get-tuple-element.11), channel_id=1, source_target_pairs={{0,16},{16,0},{1,17},{17,1},{2,18},{18,2},{3,19},{19,3},{4,20},{20... | collective-permute-start | bytes 73736 | tf_op jit(solution)/shard_map/ppermute | solution.py:20
  13.9 20.3 %collective-permute-start.1 = (bf16[896,256]{1,0:T(8,128)(2,1)}, bf16[896,256]{1,0:T(8,128)(2,1)S(1)}, u32[]{:S(2)}, u32[]{:S(2)}) collective-permute-start(bf16[896,256]{1,0:T(8,128)(2,1)} %param.13), channel_id=1, source_target_pairs={{0,16},{16,0},{1,17},{17,1},{2,18},{18,2},{3,19},{19,3},{4,20},{20... | collective-permute-start | bytes 1376264 | tf_op jit(solution)/shard_map/ppermute | solution.py:20
  34.2 2.3 %copy-start.4 = (bf16[768,512]{1,0:T(8,128)(2,1)}, bf16[768,512]{1,0:T(8,128)(2,1)S(1)}, u32[]{:S(2)}) copy-start(bf16[768,512]{1,0:T(8,128)(2,1)S(1)} %all_gather.9) | copy-start | bytes 2359300
  106.7 6.5 %copy-start.6 = (bf16[96,256]{1,0:T(8,128)(2,1)S(1)}, bf16[96,256]{1,0:T(8,128)(2,1)}, u32[]{:S(2)}) copy-start(bf16[96,256]{1,0:T(8,128)(2,1)} %param.7) | copy-start | bytes 147460
  107.9 7.7 %copy-start.7 = (bf16[256,896]{1,0:T(8,128)(2,1)S(1)}, bf16[256,896]{1,0:T(8,128)(2,1)}, u32[]{:S(2)}) copy-start(bf16[256,896]{1,0:T(8,128)(2,1)} %param.12) | copy-start | bytes 1376260
  107.9 11.1 %copy-start.8 = (bf16[256,896]{1,0:T(8,128)(2,1)S(1)}, bf16[256,896]{1,0:T(8,128)(2,1)}, u32[]{:S(2)}) copy-start(bf16[256,896]{1,0:T(8,128)(2,1)} %param.11) | copy-start | bytes 1376260
  107.9 32.1 %all-to-all-start.3 = ((bf16[4,192,896]{2,1,0:T(8,128)(2,1)}), bf16[4,192,896]{2,1,0:T(8,128)(2,1)S(1)}, u32[]{:S(2)}, u32[]{:S(2)}) async-start(bf16[4,192,896]{2,1,0:T(8,128)(2,1)} %broadcast_in_dim.15), calls=%async_computation.3 | async-start | bytes 2752512 | tf_op jit(solution)/shard_map/all_to_all | solution.py:67
  113.2 8.3 %collective-permute-start.5 = (bf16[48,256]{1,0:T(8,128)(2,1)S(1)}, bf16[48,256]{1,0:T(8,128)(2,1)S(1)}, u32[]{:S(2)}, u32[]{:S(2)}) collective-permute-start(bf16[48,256]{1,0:T(8,128)(2,1)S(1)} %get-tuple-element.7), channel_id=1, source_target_pairs={{0,16},{16,0},{1,17},{17,1},{2,18},{18,2},{3,19},{19,3},{4,20},{20... | collective-permute-start | bytes 73736 | tf_op jit(solution)/shard_map/ppermute | solution.py:20
  115.6 30.0 %collective-permute-start.3 = (bf16[256,896]{1,0:T(8,128)(2,1)S(1)}, bf16[256,896]{1,0:T(8,128)(2,1)}, u32[]{:S(2)}, u32[]{:S(2)}) collective-permute-start(bf16[256,896]{1,0:T(8,128)(2,1)S(1)} %copy-done.7), channel_id=1, source_target_pairs={{0,16},{16,0},{1,17},{17,1},{2,18},{18,2},{3,19},{19,3},{4,20},{20... | collective-permute-start | bytes 1376264 | tf_op jit(solution)/shard_map/ppermute | solution.py:20
  119.1 30.8 %collective-permute-start.2 = (bf16[256,896]{1,0:T(8,128)(2,1)S(1)}, bf16[256,896]{1,0:T(8,128)(2,1)S(1)}, u32[]{:S(2)}, u32[]{:S(2)}) collective-permute-start(bf16[256,896]{1,0:T(8,128)(2,1)S(1)} %copy-done.8), channel_id=1, source_target_pairs={{0,16},{16,0},{1,17},{17,1},{2,18},{18,2},{3,19},{19,3},{4,20},{20... | collective-permute-start | bytes 1376264 | tf_op jit(solution)/shard_map/ppermute | solution.py:20
  155.4 15.1 %copy-start = (bf16[768,1792]{1,0:T(8,128)(2,1)S(1)}, bf16[768,1792]{1,0:T(8,128)(2,1)}, u32[]{:S(2)}) copy-start(bf16[768,1792]{1,0:T(8,128)(2,1)} %all-gather.2.cloned.1.call-done) | copy-start | bytes 8257540
  156.4 33.0 %all-to-all-start.5 = ((bf16[8,48,512]{2,1,0:T(8,128)(2,1)}), bf16[8,48,512]{2,1,0:T(8,128)(2,1)S(1)}, u32[]{:S(2)}, u32[]{:S(2)}) async-start(bf16[8,48,512]{2,1,0:T(8,128)(2,1)} %reduce_sum.50), calls=%async_computation.5 | async-start | bytes 786432 | tf_op jit(solution)/shard_map/all_to_all | solution.py:38
  162.0 8.6 %copy-start.5 = (bf16[768,512]{1,0:T(8,128)(2,1)S(1)}, bf16[768,512]{1,0:T(8,128)(2,1)}, u32[]{:S(2)}) copy-start(bf16[768,512]{1,0:T(8,128)(2,1)} %copy-done.4) | copy-start | bytes 2359300
  163.3 15.3 %collective-permute-start.6 = (bf16[256,896]{1,0:T(8,128)(2,1)S(1)}, bf16[256,896]{1,0:T(8,128)(2,1)S(1)}, u32[]{:S(2)}, u32[]{:S(2)}) collective-permute-start(bf16[256,896]{1,0:T(8,128)(2,1)S(1)} %slice.79), channel_id=1, source_target_pairs={{0,16},{16,0},{1,17},{17,1},{2,18},{18,2},{3,19},{19,3},{4,20},{20... | collective-permute-start | bytes 1376264 | tf_op jit(solution)/shard_map/ppermute | solution.py:20
  168.0 10.7 %copy-start.2 = (f32[512,896]{1,0:T(8,128)S(1)}, f32[512,896]{1,0:T(8,128)}, u32[]{:S(2)}) copy-start(f32[512,896]{1,0:T(8,128)} %fusion.30) | copy-start | bytes 5505028
  168.0 20.5 %collective-permute-start.7 = (bf16[256,896]{1,0:T(8,128)(2,1)S(1)}, bf16[256,896]{1,0:T(8,128)(2,1)S(1)}, u32[]{:S(2)}, u32[]{:S(2)}) collective-permute-start(bf16[256,896]{1,0:T(8,128)(2,1)S(1)} %slice.78), channel_id=1, source_target_pairs={{0,16},{16,0},{1,17},{17,1},{2,18},{18,2},{3,19},{19,3},{4,20},{20... | collective-permute-start | bytes 1376264 | tf_op jit(solution)/shard_map/ppermute | solution.py:20
  171.5 16.9 %copy-start.3 = (f32[896,512]{1,0:T(8,128)}, f32[896,512]{1,0:T(8,128)S(1)}, u32[]{:S(2)}) copy-start(f32[896,512]{1,0:T(8,128)S(1)} %fusion.9) | copy-start | bytes 5505028
  171.5 16.9 %copy-start.1 = (f32[512,896]{1,0:T(8,128)S(1)}, f32[512,896]{1,0:T(8,128)}, u32[]{:S(2)}) copy-start(f32[512,896]{1,0:T(8,128)} %fusion.31) | copy-start | bytes 5505028
  171.6 25.5 %collective-permute-start.8 = (bf16[896,256]{1,0:T(8,128)(2,1)S(1)}, bf16[896,256]{1,0:T(8,128)(2,1)S(1)}, u32[]{:S(2)}, u32[]{:S(2)}) collective-permute-start(bf16[896,256]{1,0:T(8,128)(2,1)S(1)} %slice.77), channel_id=1, source_target_pairs={{0,16},{16,0},{1,17},{17,1},{2,18},{18,2},{3,19},{19,3},{4,20},{20... | collective-permute-start | bytes 1376264 | tf_op jit(solution)/shard_map/ppermute | solution.py:20
  189.4 9.7 %collective-permute-start.4 = (bf16[48,256]{1,0:T(8,128)(2,1)S(1)}, bf16[48,256]{1,0:T(8,128)(2,1)S(1)}, u32[]{:S(2)}, u32[]{:S(2)}) collective-permute-start(bf16[48,256]{1,0:T(8,128)(2,1)S(1)} %get-tuple-element.9), channel_id=1, source_target_pairs={{0,16},{16,0},{1,17},{17,1},{2,18},{18,2},{3,19},{19,3},{4,20},{20... | collective-permute-start | bytes 73736 | tf_op jit(solution)/shard_map/ppermute | solution.py:20
Sparse Core Ops, SparseCore 0:
  11.6 82.5 all-gather.1

commit v2 on v1

v2 whole, which is shorter than its diff:
```python
import jax
import jax.numpy as jnp
from jax import lax
from jax.sharding import Mesh, PartitionSpec as P

BF = jnp.bfloat16
F32 = jnp.float32
SWAP = [(0, 1), (1, 0)]


def contract_rows(left, right):
    return lax.dot_general(left, right, (((0,), (0,)), ((), ())), preferred_element_type=F32)


def contract_cols(left, right):
    return lax.dot_general(left, right, (((1,), (1,)), ((), ())), preferred_element_type=F32)


def swap(value):
    return lax.ppermute(value, "zw", SWAP)


def halves(value, w):
    n = value.shape[0] // 2
    return (
        lax.dynamic_slice_in_dim(value, w * n, n, 0),
        lax.dynamic_slice_in_dim(value, (1 - w) * n, n, 0),
    )


def pair_columns(value, w):
    mine, theirs = halves(value, w)
    return in_order(mine, swap(theirs), w, 1)


def spread(value, axis, parts):
    copies = jnp.broadcast_to(value[None], (parts,) + value.shape)
    return lax.all_to_all(copies, axis, 0, 0, tiled=True).reshape((-1,) + value.shape[1:])


def scatter_sum(value, axis):
    return lax.all_to_all(value, axis, 0, 0, tiled=True).astype(F32).sum(axis=0)


def in_order(own, other, index, axis):
    return jnp.where(
        index == 0,
        jnp.concatenate([own, other], axis=axis),
        jnp.concatenate([other, own], axis=axis),
    )


def tie(*values):
    return lax.optimization_barrier(values)


def body(saved_inputs, out_grad, gate_pre, up_pre, gate_weight, up_weight, down_weight):
    w = lax.axis_index("zw")
    c = lax.axis_index("core")
    width = out_grad.shape[1]
    tokens, units = gate_pre.shape

    rows = jnp.concatenate([out_grad, saved_inputs], axis=1).reshape(2, 1, tokens, 2 * width)
    rows = jnp.broadcast_to(rows, (2, 8, tokens, 2 * width)).reshape(16, tokens, 2 * width)
    rows, down_weight = tie(rows, down_weight)
    rows = lax.all_to_all(rows, ("zw", "y"), 0, 0, tiled=True)
    rows = rows.reshape(2, 8, 1, tokens, 2 * width)
    down_w = swap(down_weight)
    rows, down_w = tie(rows, down_w)
    down_w = jnp.concatenate([down_weight, down_w], axis=1)
    rows = in_order(rows, lax.ppermute(rows, "core", SWAP), c, 2)
    own, other = (
        lax.dynamic_index_in_dim(rows, i, 0, keepdims=False).reshape(16 * tokens, 2 * width)
        for i in (w, 1 - w)
    )
    grads = jnp.concatenate([own[:, :width], other[:, :width]], axis=1)

    part = contract_cols(grads, down_w).astype(BF)
    part, gate_pre, up_pre, own, other = tie(part, gate_pre, up_pre, own, other)
    pre = jnp.concatenate([gate_pre, up_pre], axis=1)
    pre = lax.all_gather(pre, "zq", axis=0, tiled=True)
    part = scatter_sum(part.reshape(4, 4 * tokens, units), "x").astype(BF)
    part, pre, gate_weight, up_weight = tie(part, pre, gate_weight, up_weight)
    pre = lax.all_gather(pre, "x", axis=0, tiled=True)
    own, other = own[:, width:], other[:, width:]
    part = scatter_sum(part.reshape(4, tokens, units), "zq").astype(BF)
    both_w = jnp.concatenate([gate_weight, up_weight], axis=1)
    part, own, other = tie(part, own, other)
    hidden_grad = spread(part, "zq", 4)
    hidden_grad, both_w = tie(hidden_grad, both_w)
    hidden_grad = spread(hidden_grad, "x", 4)
    both_w_other = swap(both_w)

    gate_val = pre[:, :units].astype(F32)
    up_val = pre[:, units:].astype(F32)
    sigma = jax.nn.sigmoid(gate_val)
    silu = gate_val * sigma
    hidden = (silu * up_val).astype(BF)
    down_other = contract_rows(hidden, grads[:, width:]).astype(BF)
    hidden_grad, down_other, pre = tie(hidden_grad, down_other, pre)
    down_other = swap(down_other)

    gate_val = pre[:, :units].astype(F32)
    up_val = pre[:, units:].astype(F32)
    sigma = jax.nn.sigmoid(gate_val)
    silu = gate_val * sigma
    hidden_grad = hidden_grad.astype(F32)
    gate_delta = hidden_grad * up_val * sigma * (1.0 + gate_val * (1.0 - sigma))
    up_delta = hidden_grad * silu
    both = jnp.concatenate([gate_delta.astype(BF), up_delta.astype(BF)], axis=1)
    sums_other = contract_rows(other, both).astype(BF)
    both, sums_other = tie(both, sums_other)
    sums_other = swap(sums_other)
    term = [contract_cols(both, m).astype(BF) for m in (both_w, both_w_other)]
    term = [t.reshape(8, 2, tokens, width).transpose(1, 0, 2, 3) for t in term]
    term = jnp.where(w == 0, jnp.stack(term, axis=1), jnp.stack(term[::-1], axis=1))
    term = lax.all_to_all(term, "core", 0, 0, tiled=True)
    term = term.astype(F32).sum(axis=0).astype(BF).reshape(16, tokens, width)
    term = lax.all_to_all(term, ("zw", "y"), 0, 0, tiled=True)
    gate_grad = (contract_rows(own, both[:, :units]) + sums_other[:, :units].astype(F32)).astype(BF)
    up_grad = (contract_rows(own, both[:, units:]) + sums_other[:, units:].astype(F32)).astype(BF)
    down_grad = (contract_rows(hidden, grads[:, :width]) + down_other.astype(F32)).astype(BF)
    term, gate_grad, up_grad = tie(term, gate_grad, up_grad)
    input_grad = term.astype(F32).reshape(2, 8, tokens, width).sum(axis=1).astype(BF)
    return (input_grad.reshape(2 * tokens, width), gate_grad, up_grad, down_grad)


def solution(mesh):
    fine = Mesh(mesh.devices.reshape(4, 4, 2, 8, 2), ("x", "zq", "zw", "y", "core"))
    row, col = ("x", "zq", "zw"), ("y", "core")
    return jax.shard_map(
        body,
        mesh=fine,
        in_specs=(
            P(col, row),
            P(col, row),
            P(row, col),
            P(row, col),
            P(row, col),
            P(row, col),
            P(col, row),
        ),
        out_specs=(P(col, row), P(row, col), P(row, col), P(col, row)),
        check_vma=False,
    )
```

time: 208 us -> 182 us (0.88)
  the two profiles are of different devices: /device:TPU:10 before, /device:TPU:8 now
where the time goes in v2:
time: 182 us; the launch traced here: 181 us
  waiting for transfers between devices  55.3 us (30%)
  starting transfers between devices  48.9 us (27%)
  blocking collectives  27.5 us (15%)
  matrix products  17.7 us (10%)
  between operations  14.3 us (8%)
  other arithmetic  10.6 us (6%)
  local copies, waits for them, and re-layouts  6.64 us (4%)
    all_gather x1, blocking collectives, body(): pre = lax.all_gather(pre, 'zq', axis=0, tiled=True)  23.1 us
    ppermute x4, waiting for transfers between devices, swap(): return lax.ppermute(value, 'zw', SWAP)  18 us
    all_to_all x2, waiting for transfers between devices, spread(): lax.all_to_all(copies, axis, 0, 0, tiled=True)  15 us
    dot_general x5, matrix products, contract_rows(): lax.dot_general(left, right, (((0,), (0,)), ((), ())), preferred_element_...  11.4 us
    ppermute x4, starting transfers between devices, swap(): return lax.ppermute(value, 'zw', SWAP)  11.3 us
    all_to_all x2, starting transfers between devices, scatter_sum(): return lax.all_to_all(value, axis, 0, 0, tiled=True).astype(F32).sum(axis=0)  10.2 us
    all_to_all x2, waiting for transfers between devices, scatter_sum(): return lax.all_to_all(value, axis, 0, 0, tiled=True).astype(F32).sum(axis=0)  9.78 us
    all_to_all x1, starting transfers between devices, body(): rows = lax.all_to_all(rows, ('zw', 'y'), 0, 0, tiled=True)  9.37 us
  transfers between devices with their start and end apart: 12, of which 8 were waited for; matrix products, arithmetic and copies ran while one was open for 15% of the time, Pallas kernels for 0%

profile of v2, /device:TPU:8, one launch (start us, length us, event | category | flops | bytes accessed | tf_op | source)
XLA Modules:
  0.0 180.9 jit_solution(7976272698257927211)
XLA Ops:
  8.9 9.4 %all-to-all-start = ((bf16[16,48,512]{2,1,0:T(8,128)(2,1)}), bf16[16,48,512]{2,1,0:T(8,128)(2,1)S(1)}, u32[]{:S(2)}, u32[]{:S(2)}) async-start(bf16[16,48,512]{2,1,0:T(8,128)(2,1)} %bitcast.1), calls=%async_computation | async-start | bytes 1572864 | tf_op jit(solution)/shard_map/all_to_all | solution.py:66
  18.3 3.4 %collective-permute-start = (bf16[896,256]{1,0:T(8,128)(2,1)}, bf16[896,256]{1,0:T(8,128)(2,1)S(1)}, u32[]{:S(2)}, u32[]{:S(2)}) collective-permute-start(bf16[896,256]{1,0:T(8,128)(2,1)} %param.13), channel_id=1, source_target_pairs={{0,16},{16,0},{1,17},{17,1},{2,18},{18,2},{3,19},{19,3},{4,20},{20... | collective-permute-start | bytes 1376264 | tf_op jit(solution)/shard_map/ppermute | solution.py:20
  21.7 17.8 %collective-permute-done = bf16[896,256]{1,0:T(8,128)(2,1)S(1)} collective-permute-done((bf16[896,256]{1,0:T(8,128)(2,1)}, bf16[896,256]{1,0:T(8,128)(2,1)S(1)}, u32[]{:S(2)}, u32[]{:S(2)}) %collective-permute-start) | collective-permute-done | bytes 458784 | tf_op jit(solution)/shard_map/ppermute | solution.py:20
  41.4 2.2 %collective-permute-done.1 = bf16[2,8,1,48,512]{4,3,2,1,0:T(8,128)(2,1)S(1)} collective-permute-done((bf16[2,8,1,48,512]{4,3,2,1,0:T(8,128)(2,1)S(1)}, bf16[2,8,1,48,512]{4,3,2,1,0:T(8,128)(2,1)S(1)}, u32[]{:S(2)}, u32[]{:S(2)}) %collective-permute-start.1) | collective-permute-done | bytes 786464 | tf_op jit(solution)/shard_map/ppermute | solution.py:71
  46.9 4.3 %all-to-all-start.1 = ((bf16[4,192,896]{2,1,0:T(8,128)(2,1)}), bf16[4,192,896]{2,1,0:T(8,128)(2,1)S(1)}, u32[]{:S(2)}, u32[]{:S(2)}) async-start(bf16[4,192,896]{2,1,0:T(8,128)(2,1)} %bitcast.40), calls=%async_computation.1 | async-start | bytes 2752512 | tf_op jit(solution)/shard_map/all_to_all | solution.py:42
  51.3 23.1 %all_gather.6 = bf16[192,1792]{1,0:T(8,128)(2,1)} all-gather(bf16[48,1792]{1,0:T(8,128)(2,1)S(1)} %pad_maximum_fusion.2), channel_id=1, replica_groups=mesh['x'=4,'zq'=4,'zw'=2,'y'=8,'core'=2] {'zq'}, dimensions={0}, use_global_device_ids=true | all-gather | bytes 860160 | tf_op jit(solution)/shard_map/all_gather | solution.py:81
  75.5 5.9 %all-to-all-start.2 = ((bf16[4,48,896]{2,1,0:T(8,128)(2,1)}), bf16[4,48,896]{2,1,0:T(8,128)(2,1)S(1)}, u32[]{:S(2)}, u32[]{:S(2)}) async-start(bf16[4,48,896]{2,1,0:T(8,128)(2,1)} %bitcast.6), calls=%async_computation.2 | async-start | bytes 688128 | tf_op jit(solution)/shard_map/all_to_all | solution.py:42
  82.9 9.8 %all-to-all-done.2 = bf16[4,48,896]{2,1,0:T(8,128)(2,1)S(1)} async-done(((bf16[4,48,896]{2,1,0:T(8,128)(2,1)}), bf16[4,48,896]{2,1,0:T(8,128)(2,1)S(1)}, u32[]{:S(2)}, u32[]{:S(2)}) %all-to-all-start.2) | async-done | bytes 344096 | tf_op jit(solution)/shard_map/all_to_all | solution.py:42
  93.5 3.5 %all-to-all-start.3 = ((bf16[4,48,896]{2,1,0:T(8,128)(2,1)}), bf16[4,48,896]{2,1,0:T(8,128)(2,1)S(1)}, u32[]{:S(2)}, u32[]{:S(2)}) async-start(bf16[4,48,896]{2,1,0:T(8,128)(2,1)} %broadcast_in_dim.10), calls=%async_computation.3 | async-start | bytes 688128 | tf_op jit(solution)/shard_map/all_to_all | solution.py:38
  98.0 9.5 %all-to-all-done.3 = bf16[4,48,896]{2,1,0:T(8,128)(2,1)S(1)} async-done(((bf16[4,48,896]{2,1,0:T(8,128)(2,1)}), bf16[4,48,896]{2,1,0:T(8,128)(2,1)S(1)}, u32[]{:S(2)}, u32[]{:S(2)}) %all-to-all-start.3) | async-done | bytes 344096 | tf_op jit(solution)/shard_map/all_to_all | solution.py:38
  108.7 4.3 %all-to-all-start.4 = ((bf16[4,192,896]{2,1,0:T(8,128)(2,1)}), bf16[4,192,896]{2,1,0:T(8,128)(2,1)}, u32[]{:S(2)}, u32[]{:S(2)}) async-start(bf16[4,192,896]{2,1,0:T(8,128)(2,1)} %broadcast_in_dim.22), calls=%async_computation.4 | async-start | bytes 2752512 | tf_op jit(solution)/shard_map/all_to_all | solution.py:38
  115.0 4.8 %all-gather.2.cloned.1.call-done = bf16[768,1792]{1,0:T(8,128)(2,1)} async-done(((bf16[192,1792]{1,0:T(8,128)(2,1)}), bf16[768,1792]{1,0:T(8,128)(2,1)}) %all-gather.2.cloned.1.call-update) | async-done | bytes 2752528 | tf_op jit(solution)/shard_map/all_gather | solution.py:84
  119.8 2.7 %fusion.12 = bf16[768,896]{1,0:T(8,128)(2,1)S(1)} fusion(bf16[768,1792]{1,0:T(8,128)(2,1)} %all-gather.2.cloned.1.call-done), kind=kLoop, calls=%fused_computation.20 | loop fusion | flops 5505024 | bytes 4128768 | tf_op jit(solution)/shard_map/convert_element_type | solution.py:98
  123.6 2.3 %convolution_convert_fusion.2 = bf16[896,256]{1,0:T(8,128)(2,1)} fusion(bf16[768,896]{1,0:T(8,128)(2,1)S(1)} %fusion.12, bf16[768,512]{1,0:T(8,128)(2,1)} %bitcast.37), kind=kOutput, calls=%fused_computation.28 | convolution fusion | flops 352550912 | bytes 2228224 | tf_op jit(solution)/shard_map/dot_general | solution.py:12
  126.0 5.6 %all-to-all-done.4 = bf16[4,192,896]{2,1,0:T(8,128)(2,1)} async-done(((bf16[4,192,896]{2,1,0:T(8,128)(2,1)}), bf16[4,192,896]{2,1,0:T(8,128)(2,1)}, u32[]{:S(2)}, u32[]{:S(2)}) %all-to-all-start.4) | async-done | bytes 1376288 | tf_op jit(solution)/shard_map/all_to_all | solution.py:38
  131.5 3.7 %collective-permute-start.4 = (bf16[896,256]{1,0:T(8,128)(2,1)}, bf16[896,256]{1,0:T(8,128)(2,1)}, u32[]{:S(2)}, u32[]{:S(2)}) collective-permute-start(bf16[896,256]{1,0:T(8,128)(2,1)} %convolution_convert_fusion.2), channel_id=1, source_target_pairs={{0,16},{16,0},{1,17},{17,1},{2,18},{18,2},{3,19},{19,3},{4,20},{20... | collective-permute-start | bytes 1376264 | tf_op jit(solution)/shard_map/ppermute | solution.py:20
  135.2 2.8 %fusion.6 = (bf16[768,896]{1,0:T(8,128)(2,1)S(1)}, bf16[768,896]{1,0:T(8,128)(2,1)S(1)}) fusion(bf16[768,896]{1,0:T(8,128)(2,1)} %bitcast.8, bf16[768,1792]{1,0:T(8,128)(2,1)S(1)} %copy-done), kind=kLoop, calls=%fused_computation.13 | loop fusion | flops 11010048 | bytes 6881280 | tf_op jit(solution)/shard_map/convert_element_type | solution.py:110
  140.1 2.3 %collective-permute-start.3 = (bf16[256,1792]{1,0:T(8,128)(2,1)}, bf16[256,1792]{1,0:T(8,128)(2,1)}, u32[]{:S(2)}, u32[]{:S(2)}) collective-permute-start(bf16[256,1792]{1,0:T(8,128)(2,1)} %convolution_convert_fusion), channel_id=1, source_target_pairs={{0,16},{16,0},{1,17},{17,1},{2,18},{18,2},{3,19},{19,3},{4,20},{20... | collective-permute-start | bytes 2752520 | tf_op jit(solution)/shard_map/ppermute | solution.py:20
  146.8 4.4 %all_to_all.35 = bf16[2,2,8,48,256]{4,3,2,1,0:T(8,128)(2,1)S(1)} all-to-all(bf16[2,2,8,48,256]{4,3,2,1,0:T(8,128)(2,1)S(1)} %maximum_select_fusion.1), channel_id=1, replica_groups=mesh['x'=4,'zq'=4,'zw'=2,'y'=8,'core'=2] {'core'}, dimensions={0} | all-to-all | bytes 1572864 | tf_op jit(solution)/shard_map/all_to_all | solution.py:117
  152.2 8.4 %all-to-all-start.6 = ((bf16[16,48,256]{2,1,0:T(8,128)(2,1)}), bf16[16,48,256]{2,1,0:T(8,128)(2,1)S(1)}, u32[]{:S(2)}, u32[]{:S(2)}) async-start(bf16[16,48,256]{2,1,0:T(8,128)(2,1)} %bitcast.17), calls=%async_computation.6 | async-start | bytes 786432 | tf_op jit(solution)/shard_map/all_to_all | solution.py:119
  160.5 2.2 %fusion.15 = f32[256,896]{1,0:T(8,128)S(1)} fusion(bf16[768,256]{1,0:T(8,128)(2,1)} %slice.38, bf16[768,1792]{1,0:T(8,128)(2,1)} %copy-done.2), kind=kOutput, calls=%fused_computation.26 | convolution fusion | flops 352321536 | bytes 2686976 | tf_op jit(solution)/shard_map/dot_general | solution.py:12
  162.8 2.4 %add_convert_fusion = bf16[896,256]{1,0:T(8,128)(2,1)} fusion(bf16[896,256]{1,0:T(8,128)(2,1)} %collective-permute-done.4, bf16[768,896]{1,0:T(8,128)(2,1)S(1)} %copy-done.5, bf16[768,512]{1,0:T(8,128)(2,1)S(1)} %bitcast.34), kind=kOutput, calls=%fused_computation.35 | convolution fusion | flops 353009664 | bytes 2686976 | tf_op jit(solution)/shard_map/dot_general | solution.py:12
  165.4 2.7 %add_convert_fusion.1 = (bf16[256,896]{1,0:T(8,128)(2,1)}, bf16[256,896]{1,0:T(8,128)(2,1)}) fusion(bf16[256,1792]{1,0:T(8,128)(2,1)} %collective-permute-done.3, f32[256,896]{1,0:T(8,128)S(1)} %fusion.15, bf16[768,256]{1,0:T(8,128)(2,1)S(1)} %copy-done.8, bf16[768,1792]{1,0:T(8,128)(2,1)S(1)} %copy-done.3), kind=kOutput, calls=%fused_computation.36 | convolution fusion | flops 353697792 | bytes 4521984 | tf_op jit(solution)/shard_map/dot_general | solution.py:12
  168.1 5.3 %all-to-all-done.6 = bf16[16,48,256]{2,1,0:T(8,128)(2,1)S(1)} async-done(((bf16[16,48,256]{2,1,0:T(8,128)(2,1)}), bf16[16,48,256]{2,1,0:T(8,128)(2,1)S(1)}, u32[]{:S(2)}, u32[]{:S(2)}) %all-to-all-start.6) | async-done | bytes 393248 | tf_op jit(solution)/shard_map/all_to_all | solution.py:119
  (58 shorter events, 23.9 us)
Async XLA Ops:
  8.9 30.5 %all-to-all-start = ((bf16[16,48,512]{2,1,0:T(8,128)(2,1)}), bf16[16,48,512]{2,1,0:T(8,128)(2,1)S(1)}, u32[]{:S(2)}, u32[]{:S(2)}) async-start(bf16[16,48,512]{2,1,0:T(8,128)(2,1)} %bitcast.1), calls=%async_computation | async-start | bytes 1572864 | tf_op jit(solution)/shard_map/all_to_all | solution.py:66
  18.3 21.2 %collective-permute-start = (bf16[896,256]{1,0:T(8,128)(2,1)}, bf16[896,256]{1,0:T(8,128)(2,1)S(1)}, u32[]{:S(2)}, u32[]{:S(2)}) collective-permute-start(bf16[896,256]{1,0:T(8,128)(2,1)} %param.13), channel_id=1, source_target_pairs={{0,16},{16,0},{1,17},{17,1},{2,18},{18,2},{3,19},{19,3},{4,20},{20... | collective-permute-start | bytes 1376264 | tf_op jit(solution)/shard_map/ppermute | solution.py:20
  39.5 4.2 %collective-permute-start.1 = (bf16[2,8,1,48,512]{4,3,2,1,0:T(8,128)(2,1)S(1)}, bf16[2,8,1,48,512]{4,3,2,1,0:T(8,128)(2,1)S(1)}, u32[]{:S(2)}, u32[]{:S(2)}) collective-permute-start(bf16[2,8,1,48,512]{4,3,2,1,0:T(8,128)(2,1)S(1)} %bitcast.38), channel_id=1, source_target_pairs={{0,1},{1,0},{2,3},{3,2},{4,5},{5,4},{6,7},{7,6},{8,9},{9,8},{10,11... | collective-permute-start | bytes 2359304 | tf_op jit(solution)/shard_map/ppermute | solution.py:71
  44.0 38.2 %copy-start.1 = (bf16[1,8,2,48,512]{4,3,2,1,0:T(8,128)(2,1)}, bf16[1,8,2,48,512]{4,3,2,1,0:T(8,128)(2,1)S(1)}, u32[]{:S(2)}) copy-start(bf16[1,8,2,48,512]{4,3,2,1,0:T(8,128)(2,1)S(1)} %get-tuple-element.59) | copy-start | bytes 2359300
  44.8 6.4 %copy-start.10 = (bf16[48,896]{1,0:T(8,128)(2,1)S(1)}, bf16[48,896]{1,0:T(8,128)(2,1)}, u32[]{:S(2)}) copy-start(bf16[48,896]{1,0:T(8,128)(2,1)} %param.10) | copy-start | bytes 258052
  44.8 6.4 %copy-start.11 = (bf16[48,896]{1,0:T(8,128)(2,1)S(1)}, bf16[48,896]{1,0:T(8,128)(2,1)}, u32[]{:S(2)}) copy-start(bf16[48,896]{1,0:T(8,128)(2,1)} %param.9) | copy-start | bytes 258052
  46.9 27.5 %all-to-all-start.1 = ((bf16[4,192,896]{2,1,0:T(8,128)(2,1)}), bf16[4,192,896]{2,1,0:T(8,128)(2,1)S(1)}, u32[]{:S(2)}, u32[]{:S(2)}) async-start(bf16[4,192,896]{2,1,0:T(8,128)(2,1)} %bitcast.40), calls=%async_computation.1 | async-start | bytes 2752512 | tf_op jit(solution)/shard_map/all_to_all | solution.py:42
  51.2 68.5 %all-gather.2.cloned.1.call-start = ((), (), s32[]{:S(2)}) async-start(), calls=%async_computation.7 | async-start | bytes 3440640 | tf_op jit(solution)/shard_map/all_gather | solution.py:84
  74.4 22.6 %copy-start.6 = (bf16[256,896]{1,0:T(8,128)(2,1)S(1)}, bf16[256,896]{1,0:T(8,128)(2,1)}, u32[]{:S(2)}) copy-start(bf16[256,896]{1,0:T(8,128)(2,1)} %param.12) | copy-start | bytes 1376260
  75.4 21.6 %copy-start.7 = (bf16[256,896]{1,0:T(8,128)(2,1)S(1)}, bf16[256,896]{1,0:T(8,128)(2,1)}, u32[]{:S(2)}) copy-start(bf16[256,896]{1,0:T(8,128)(2,1)} %param.11) | copy-start | bytes 1376260
  75.5 17.3 %all-to-all-start.2 = ((bf16[4,48,896]{2,1,0:T(8,128)(2,1)}), bf16[4,48,896]{2,1,0:T(8,128)(2,1)S(1)}, u32[]{:S(2)}, u32[]{:S(2)}) async-start(bf16[4,48,896]{2,1,0:T(8,128)(2,1)} %bitcast.6), calls=%async_computation.2 | async-start | bytes 688128 | tf_op jit(solution)/shard_map/all_to_all | solution.py:42
  93.5 14.0 %all-to-all-start.3 = ((bf16[4,48,896]{2,1,0:T(8,128)(2,1)}), bf16[4,48,896]{2,1,0:T(8,128)(2,1)S(1)}, u32[]{:S(2)}, u32[]{:S(2)}) async-start(bf16[4,48,896]{2,1,0:T(8,128)(2,1)} %broadcast_in_dim.10), calls=%async_computation.3 | async-start | bytes 688128 | tf_op jit(solution)/shard_map/all_to_all | solution.py:38
  108.7 22.8 %all-to-all-start.4 = ((bf16[4,192,896]{2,1,0:T(8,128)(2,1)}), bf16[4,192,896]{2,1,0:T(8,128)(2,1)}, u32[]{:S(2)}, u32[]{:S(2)}) async-start(bf16[4,192,896]{2,1,0:T(8,128)(2,1)} %broadcast_in_dim.22), calls=%async_computation.4 | async-start | bytes 2752512 | tf_op jit(solution)/shard_map/all_to_all | solution.py:38
  113.1 31.5 %collective-permute-start.2 = (bf16[256,1792]{1,0:T(8,128)(2,1)}, bf16[256,1792]{1,0:T(8,128)(2,1)}, u32[]{:S(2)}, u32[]{:S(2)}) collective-permute-start(bf16[256,1792]{1,0:T(8,128)(2,1)} %pad_maximum_fusion.1), channel_id=1, source_target_pairs={{0,16},{16,0},{1,17},{17,1},{2,18},{18,2},{3,19},{19,3},{4,20},{20... | collective-permute-start | bytes 2752520 | tf_op jit(solution)/shard_map/ppermute | solution.py:20
  119.8 15.4 %copy-start = (bf16[768,1792]{1,0:T(8,128)(2,1)S(1)}, bf16[768,1792]{1,0:T(8,128)(2,1)}, u32[]{:S(2)}) copy-start(bf16[768,1792]{1,0:T(8,128)(2,1)} %all-gather.2.cloned.1.call-done) | copy-start | bytes 8257540
  122.5 1.1 copy-start.4
  131.5 6.5 %copy-start.9 = (bf16[768,256]{1,0:T(8,128)(2,1)S(1)}, bf16[768,256]{1,0:T(8,128)(2,1)}, u32[]{:S(2)}) copy-start(bf16[768,256]{1,0:T(8,128)(2,1)} %slice.39) | copy-start | bytes 1179652
  131.5 31.2 %collective-permute-start.4 = (bf16[896,256]{1,0:T(8,128)(2,1)}, bf16[896,256]{1,0:T(8,128)(2,1)}, u32[]{:S(2)}, u32[]{:S(2)}) collective-permute-start(bf16[896,256]{1,0:T(8,128)(2,1)} %convolution_convert_fusion.2), channel_id=1, source_target_pairs={{0,16},{16,0},{1,17},{17,1},{2,18},{18,2},{3,19},{19,3},{4,20},{20... | collective-permute-start | bytes 1376264 | tf_op jit(solution)/shard_map/ppermute | solution.py:20
  140.1 4.4 %copy-start.2 = (bf16[768,1792]{1,0:T(8,128)(2,1)}, bf16[768,1792]{1,0:T(8,128)(2,1)S(1)}, u32[]{:S(2)}) copy-start(bf16[768,1792]{1,0:T(8,128)(2,1)S(1)} %pad_maximum_fusion) | copy-start | bytes 8257540
  140.1 25.3 %collective-permute-start.3 = (bf16[256,1792]{1,0:T(8,128)(2,1)}, bf16[256,1792]{1,0:T(8,128)(2,1)}, u32[]{:S(2)}, u32[]{:S(2)}) collective-permute-start(bf16[256,1792]{1,0:T(8,128)(2,1)} %convolution_convert_fusion), channel_id=1, source_target_pairs={{0,16},{16,0},{1,17},{17,1},{2,18},{18,2},{3,19},{19,3},{4,20},{20... | collective-permute-start | bytes 2752520 | tf_op jit(solution)/shard_map/ppermute | solution.py:20
  151.2 11.6 %copy-start.5 = (bf16[768,896]{1,0:T(8,128)(2,1)S(1)}, bf16[768,896]{1,0:T(8,128)(2,1)}, u32[]{:S(2)}) copy-start(bf16[768,896]{1,0:T(8,128)(2,1)} %copy-done.4) | copy-start | bytes 4128772
  152.2 21.2 %all-to-all-start.6 = ((bf16[16,48,256]{2,1,0:T(8,128)(2,1)}), bf16[16,48,256]{2,1,0:T(8,128)(2,1)S(1)}, u32[]{:S(2)}, u32[]{:S(2)}) async-start(bf16[16,48,256]{2,1,0:T(8,128)(2,1)} %bitcast.17), calls=%async_computation.6 | async-start | bytes 786432 | tf_op jit(solution)/shard_map/all_to_all | solution.py:119
  160.5 4.9 %copy-start.3 = (bf16[768,1792]{1,0:T(8,128)(2,1)S(1)}, bf16[768,1792]{1,0:T(8,128)(2,1)}, u32[]{:S(2)}) copy-start(bf16[768,1792]{1,0:T(8,128)(2,1)} %copy-done.2) | copy-start | bytes 8257540
  160.5 4.8 %copy-start.8 = (bf16[768,256]{1,0:T(8,128)(2,1)S(1)}, bf16[768,256]{1,0:T(8,128)(2,1)}, u32[]{:S(2)}) copy-start(bf16[768,256]{1,0:T(8,128)(2,1)} %slice.38) | copy-start | bytes 1179652
  (1 other events, 1.0 us)
Sparse Core Ops, SparseCore 0:
  75.6 44.1 all-gather.1

commit v3 on v2

--- a/solution.py
+++ b/solution.py
@@ -36,6 +36,22 @@
 def spread(value, axis, parts):
     copies = jnp.broadcast_to(value[None], (parts,) + value.shape)
     return lax.all_to_all(copies, axis, 0, 0, tiled=True).reshape((-1,) + value.shape[1:])
+
+
+def pieces(value, axis, parts):
+    up = [(i, (i + 1) % parts) for i in range(parts)]
+    down = [(i, (i + parts - 1) % parts) for i in range(parts)]
+    before = lax.ppermute(value, axis, up)
+    after = lax.ppermute(value, axis, down)
+    return [before, lax.ppermute(after, axis, down), after]
+
+
+def assemble(value, others, axis):
+    me, parts = lax.axis_index(axis), len(others) + 1
+    out = jnp.zeros((parts,) + value.shape, value.dtype)
+    for k, piece in enumerate([value] + others):
+        out = lax.dynamic_update_index_in_dim(out, piece, (me + parts - k) % parts, 0)
+    return out.reshape((-1,) + value.shape[1:])
 
 
 def scatter_sum(value, axis):
@@ -81,16 +97,17 @@
     pre = lax.all_gather(pre, "zq", axis=0, tiled=True)
     part = scatter_sum(part.reshape(4, 4 * tokens, units), "x").astype(BF)
     part, pre, gate_weight, up_weight = tie(part, pre, gate_weight, up_weight)
-    pre = lax.all_gather(pre, "x", axis=0, tiled=True)
+    pre_pieces = pieces(pre, "x", 4)
     own, other = own[:, width:], other[:, width:]
     part = scatter_sum(part.reshape(4, tokens, units), "zq").astype(BF)
     both_w = jnp.concatenate([gate_weight, up_weight], axis=1)
     part, own, other = tie(part, own, other)
     hidden_grad = spread(part, "zq", 4)
-    hidden_grad, both_w = tie(hidden_grad, both_w)
+    hidden_grad, both_w, pre = tie(hidden_grad, both_w, pre)
     hidden_grad = spread(hidden_grad, "x", 4)
     both_w_other = swap(both_w)
 
+    pre = assemble(pre, pre_pieces, "x")
     gate_val = pre[:, :units].astype(F32)
     up_val = pre[:, units:].astype(F32)
     sigma = jax.nn.sigmoid(gate_val)

time: 182 us -> 169 us (0.929)
  the two profiles are of different devices: /device:TPU:8 before, /device:TPU:14 now
where the time goes in v3:
time: 169 us; the launch traced here: 168 us
  starting transfers between devices  59.9 us (35%)
  waiting for transfers between devices  42.7 us (25%)
  blocking collectives  27.4 us (16%)
  matrix products  16.8 us (10%)
  local copies, waits for them, and re-layouts  11.5 us (7%)
  other arithmetic  8.63 us (5%)
    all_gather x1, blocking collectives, body(): pre = lax.all_gather(pre, 'zq', axis=0, tiled=True)  23.1 us
    ppermute x4, waiting for transfers between devices, swap(): return lax.ppermute(value, 'zw', SWAP)  17.8 us
    ppermute x4, starting transfers between devices, swap(): return lax.ppermute(value, 'zw', SWAP)  11.2 us
    dot_general x5, matrix products, contract_rows(): lax.dot_general(left, right, (((0,), (0,)), ((), ())), preferred_element_...  10.5 us
    all_to_all x2, starting transfers between devices, scatter_sum(): return lax.all_to_all(value, axis, 0, 0, tiled=True).astype(F32).sum(axis=0)  10.4 us
    all_to_all x2, starting transfers between devices, spread(): lax.all_to_all(copies, axis, 0, 0, tiled=True)  10.3 us
    all_to_all x1, starting transfers between devices, body(): rows = lax.all_to_all(rows, ('zw', 'y'), 0, 0, tiled=True)  9.37 us
    all_to_all x1, starting transfers between devices, body(): term = lax.all_to_all(term, ('zw', 'y'), 0, 0, tiled=True)  8.21 us
  transfers between devices with their start and end apart: 14, of which 7 were waited for; matrix products, arithmetic and copies ran while one was open for 17% of the time, Pallas kernels for 0%

profile of v3, /device:TPU:14, one launch (start us, length us, event | category | flops | bytes accessed | tf_op | source)
XLA Modules:
  0.0 167.9 jit_solution(12165855184721297894)
XLA Ops:
  2.4 9.4 %all-to-all-start = ((bf16[16,48,512]{2,1,0:T(8,128)(2,1)}), bf16[16,48,512]{2,1,0:T(8,128)(2,1)S(1)}, u32[]{:S(2)}, u32[]{:S(2)}) async-start(bf16[16,48,512]{2,1,0:T(8,128)(2,1)} %bitcast.1), calls=%async_computation | async-start | bytes 1572864 | tf_op jit(solution)/shard_map/all_to_all | solution.py:82
  11.8 3.4 %collective-permute-start = (bf16[896,256]{1,0:T(8,128)(2,1)}, bf16[896,256]{1,0:T(8,128)(2,1)S(1)}, u32[]{:S(2)}, u32[]{:S(2)}) collective-permute-start(bf16[896,256]{1,0:T(8,128)(2,1)} %param.13), channel_id=1, source_target_pairs={{0,16},{16,0},{1,17},{17,1},{2,18},{18,2},{3,19},{19,3},{4,20},{20... | collective-permute-start | bytes 1376264 | tf_op jit(solution)/shard_map/ppermute | solution.py:20
  15.2 17.8 %collective-permute-done = bf16[896,256]{1,0:T(8,128)(2,1)S(1)} collective-permute-done((bf16[896,256]{1,0:T(8,128)(2,1)}, bf16[896,256]{1,0:T(8,128)(2,1)S(1)}, u32[]{:S(2)}, u32[]{:S(2)}) %collective-permute-start) | collective-permute-done | bytes 458784 | tf_op jit(solution)/shard_map/ppermute | solution.py:20
  34.9 2.2 %collective-permute-done.1 = bf16[2,8,1,48,512]{4,3,2,1,0:T(8,128)(2,1)S(1)} collective-permute-done((bf16[2,8,1,48,512]{4,3,2,1,0:T(8,128)(2,1)S(1)}, bf16[2,8,1,48,512]{4,3,2,1,0:T(8,128)(2,1)S(1)}, u32[]{:S(2)}, u32[]{:S(2)}) %collective-permute-start.1) | collective-permute-done | bytes 786464 | tf_op jit(solution)/shard_map/ppermute | solution.py:87
  38.3 2.1 %convolution_convert_fusion.1 = bf16[768,896]{1,0:T(8,128)(2,1)} fusion(bf16[896,256]{1,0:T(8,128)(2,1)S(1)} %collective-permute-done, bf16[896,256]{1,0:T(8,128)(2,1)S(1)} %copy-done.12, bf16[768,256]{1,0:T(8,128)(2,1)S(1)} %slice.49, bf16[768,256]{1,0:T(8,128)(2,1)S(1)} %slice.48), kind=kOutput, calls=%fused_computation.22 | convolution fusion | flops 708739072 | bytes 3080192 | tf_op jit(solution)/shard_map/dot_general | solution.py:16
  40.4 4.8 %all-to-all-start.1 = ((bf16[4,192,896]{2,1,0:T(8,128)(2,1)}), bf16[4,192,896]{2,1,0:T(8,128)(2,1)S(1)}, u32[]{:S(2)}, u32[]{:S(2)}) async-start(bf16[4,192,896]{2,1,0:T(8,128)(2,1)} %bitcast.51), calls=%async_computation.1 | async-start | bytes 2752512 | tf_op jit(solution)/shard_map/all_to_all | solution.py:58
  45.2 23.1 %all_gather.3 = bf16[192,1792]{1,0:T(8,128)(2,1)} all-gather(bf16[48,1792]{1,0:T(8,128)(2,1)S(1)} %pad_maximum_fusion.2), channel_id=1, replica_groups=mesh['x'=4,'zq'=4,'zw'=2,'y'=8,'core'=2] {'zq'}, dimensions={0}, use_global_device_ids=true | all-gather | bytes 860160 | tf_op jit(solution)/shard_map/all_gather | solution.py:97
  69.3 5.6 %all-to-all-start.2 = ((bf16[4,48,896]{2,1,0:T(8,128)(2,1)}), bf16[4,48,896]{2,1,0:T(8,128)(2,1)S(1)}, u32[]{:S(2)}, u32[]{:S(2)}) async-start(bf16[4,48,896]{2,1,0:T(8,128)(2,1)} %bitcast.6), calls=%async_computation.2 | async-start | bytes 688128 | tf_op jit(solution)/shard_map/all_to_all | solution.py:58
  74.9 2.6 %collective-permute-start.3 = (bf16[192,1792]{1,0:T(8,128)(2,1)}, bf16[192,1792]{1,0:T(8,128)(2,1)}, u32[]{:S(2)}, u32[]{:S(2)}) collective-permute-start(bf16[192,1792]{1,0:T(8,128)(2,1)} %all_gather.3), channel_id=1, source_target_pairs={{0,384},{128,0},{256,128},{384,256},{1,385},{129,1},{257,129},{385... | collective-permute-start | bytes 2064392 | tf_op jit(solution)/shard_map/ppermute | solution.py:45
  79.1 5.4 %all-to-all-done.2 = bf16[4,48,896]{2,1,0:T(8,128)(2,1)S(1)} async-done(((bf16[4,48,896]{2,1,0:T(8,128)(2,1)}), bf16[4,48,896]{2,1,0:T(8,128)(2,1)S(1)}, u32[]{:S(2)}, u32[]{:S(2)}) %all-to-all-start.2) | async-done | bytes 344096 | tf_op jit(solution)/shard_map/all_to_all | solution.py:58
  85.3 3.6 %all-to-all-start.3 = ((bf16[4,48,896]{2,1,0:T(8,128)(2,1)}), bf16[4,48,896]{2,1,0:T(8,128)(2,1)S(1)}, u32[]{:S(2)}, u32[]{:S(2)}) async-start(bf16[4,48,896]{2,1,0:T(8,128)(2,1)} %broadcast_in_dim.37), calls=%async_computation.3 | async-start | bytes 688128 | tf_op jit(solution)/shard_map/all_to_all | solution.py:38
  88.9 4.0 %collective-permute-start.2 = (bf16[192,1792]{1,0:T(8,128)(2,1)}, bf16[192,1792]{1,0:T(8,128)(2,1)}, u32[]{:S(2)}, u32[]{:S(2)}) collective-permute-start(bf16[192,1792]{1,0:T(8,128)(2,1)} %all_gather.3), channel_id=1, source_target_pairs={{0,128},{128,256},{256,384},{384,0},{1,129},{129,257},{257,385},{3... | collective-permute-start | bytes 2064392 | tf_op jit(solution)/shard_map/ppermute | solution.py:44
  95.8 3.2 %all-to-all-done.3 = bf16[4,48,896]{2,1,0:T(8,128)(2,1)S(1)} async-done(((bf16[4,48,896]{2,1,0:T(8,128)(2,1)}), bf16[4,48,896]{2,1,0:T(8,128)(2,1)S(1)}, u32[]{:S(2)}, u32[]{:S(2)}) %all-to-all-start.3) | async-done | bytes 344096 | tf_op jit(solution)/shard_map/all_to_all | solution.py:38
  100.2 6.7 %all-to-all-start.4 = ((bf16[4,192,896]{2,1,0:T(8,128)(2,1)}), bf16[4,192,896]{2,1,0:T(8,128)(2,1)}, u32[]{:S(2)}, u32[]{:S(2)}) async-start(bf16[4,192,896]{2,1,0:T(8,128)(2,1)} %broadcast_in_dim.38), calls=%async_computation.4 | async-start | bytes 2752512 | tf_op jit(solution)/shard_map/all_to_all | solution.py:38
  111.3 6.5 %collective-permute-done.4 = bf16[192,1792]{1,0:T(8,128)(2,1)} collective-permute-done((bf16[192,1792]{1,0:T(8,128)(2,1)}, bf16[192,1792]{1,0:T(8,128)(2,1)}, u32[]{:S(2)}, u32[]{:S(2)}) %collective-permute-start.4) | collective-permute-done | bytes 688160 | tf_op jit(solution)/shard_map/ppermute | solution.py:46
  125.5 3.1 %collective-permute-start.7 = (bf16[896,256]{1,0:T(8,128)(2,1)}, bf16[896,256]{1,0:T(8,128)(2,1)}, u32[]{:S(2)}, u32[]{:S(2)}) collective-permute-start(bf16[896,256]{1,0:T(8,128)(2,1)} %convolution_convert_fusion.2), channel_id=1, source_target_pairs={{0,16},{16,0},{1,17},{17,1},{2,18},{18,2},{3,19},{19,3},{4,20},{20... | collective-permute-start | bytes 1376264 | tf_op jit(solution)/shard_map/ppermute | solution.py:20
  128.6 2.8 %fusion.6 = (bf16[768,896]{1,0:T(8,128)(2,1)S(1)}, bf16[768,896]{1,0:T(8,128)(2,1)S(1)}) fusion(bf16[768,896]{1,0:T(8,128)(2,1)} %bitcast.8, bf16[768,1792]{1,0:T(8,128)(2,1)S(1)} %bitcast.42), kind=kLoop, calls=%fused_computation.13 | loop fusion | flops 11010048 | bytes 6881280 | tf_op jit(solution)/shard_map/convert_element_type | solution.py:127
  133.5 2.9 %collective-permute-start.6 = (bf16[256,1792]{1,0:T(8,128)(2,1)}, bf16[256,1792]{1,0:T(8,128)(2,1)}, u32[]{:S(2)}, u32[]{:S(2)}) collective-permute-start(bf16[256,1792]{1,0:T(8,128)(2,1)} %convolution_convert_fusion), channel_id=1, source_target_pairs={{0,16},{16,0},{1,17},{17,1},{2,18},{18,2},{3,19},{19,3},{4,20},{20... | collective-permute-start | bytes 2752520 | tf_op jit(solution)/shard_map/ppermute | solution.py:20
  140.8 4.4 %all_to_all.35 = bf16[2,2,8,48,256]{4,3,2,1,0:T(8,128)(2,1)S(1)} all-to-all(bf16[2,2,8,48,256]{4,3,2,1,0:T(8,128)(2,1)S(1)} %maximum_select_fusion.1), channel_id=1, replica_groups=mesh['x'=4,'zq'=4,'zw'=2,'y'=8,'core'=2] {'core'}, dimensions={0} | all-to-all | bytes 1572864 | tf_op jit(solution)/shard_map/all_to_all | solution.py:134
  146.1 8.2 %all-to-all-start.6 = ((bf16[16,48,256]{2,1,0:T(8,128)(2,1)}), bf16[16,48,256]{2,1,0:T(8,128)(2,1)S(1)}, u32[]{:S(2)}, u32[]{:S(2)}) async-start(bf16[16,48,256]{2,1,0:T(8,128)(2,1)} %bitcast.22), calls=%async_computation.6 | async-start | bytes 786432 | tf_op jit(solution)/shard_map/all_to_all | solution.py:136
  154.3 2.2 %fusion.15 = f32[256,896]{1,0:T(8,128)S(1)} fusion(bf16[768,256]{1,0:T(8,128)(2,1)} %slice.38, bf16[768,1792]{1,0:T(8,128)(2,1)} %copy-done.2), kind=kOutput, calls=%fused_computation.26 | convolution fusion | flops 352321536 | bytes 2686976 | tf_op jit(solution)/shard_map/dot_general | solution.py:12
  156.6 2.4 %add_convert_fusion = bf16[896,256]{1,0:T(8,128)(2,1)} fusion(bf16[896,256]{1,0:T(8,128)(2,1)} %collective-permute-done.7, bf16[768,896]{1,0:T(8,128)(2,1)S(1)} %copy-done.5, bf16[768,512]{1,0:T(8,128)(2,1)S(1)} %bitcast.45), kind=kOutput, calls=%fused_computation.35 | convolution fusion | flops 353009664 | bytes 2686976 | tf_op jit(solution)/shard_map/dot_general | solution.py:12
  158.9 2.7 %add_convert_fusion.1 = (bf16[256,896]{1,0:T(8,128)(2,1)}, bf16[256,896]{1,0:T(8,128)(2,1)}) fusion(bf16[256,1792]{1,0:T(8,128)(2,1)} %collective-permute-done.6, f32[256,896]{1,0:T(8,128)S(1)} %fusion.15, bf16[768,256]{1,0:T(8,128)(2,1)S(1)} %copy-done.8, bf16[768,1792]{1,0:T(8,128)(2,1)S(1)} %copy-done.3), kind=kOutput, calls=%fused_computation.36 | convolution fusion | flops 353697792 | bytes 4521984 | tf_op jit(solution)/shard_map/dot_general | solution.py:12
  161.7 5.5 %all-to-all-done.6 = bf16[16,48,256]{2,1,0:T(8,128)(2,1)S(1)} async-done(((bf16[16,48,256]{2,1,0:T(8,128)(2,1)}), bf16[16,48,256]{2,1,0:T(8,128)(2,1)S(1)}, u32[]{:S(2)}, u32[]{:S(2)}) %all-to-all-start.6) | async-done | bytes 393248 | tf_op jit(solution)/shard_map/all_to_all | solution.py:136
  (66 shorter events, 32.5 us)
Async XLA Ops:
  2.4 30.5 %all-to-all-start = ((bf16[16,48,512]{2,1,0:T(8,128)(2,1)}), bf16[16,48,512]{2,1,0:T(8,128)(2,1)S(1)}, u32[]{:S(2)}, u32[]{:S(2)}) async-start(bf16[16,48,512]{2,1,0:T(8,128)(2,1)} %bitcast.1), calls=%async_computation | async-start | bytes 1572864 | tf_op jit(solution)/shard_map/all_to_all | solution.py:82
  11.8 21.2 %collective-permute-start = (bf16[896,256]{1,0:T(8,128)(2,1)}, bf16[896,256]{1,0:T(8,128)(2,1)S(1)}, u32[]{:S(2)}, u32[]{:S(2)}) collective-permute-start(bf16[896,256]{1,0:T(8,128)(2,1)} %param.13), channel_id=1, source_target_pairs={{0,16},{16,0},{1,17},{17,1},{2,18},{18,2},{3,19},{19,3},{4,20},{20... | collective-permute-start | bytes 1376264 | tf_op jit(solution)/shard_map/ppermute | solution.py:20
  33.0 4.2 %collective-permute-start.1 = (bf16[2,8,1,48,512]{4,3,2,1,0:T(8,128)(2,1)S(1)}, bf16[2,8,1,48,512]{4,3,2,1,0:T(8,128)(2,1)S(1)}, u32[]{:S(2)}, u32[]{:S(2)}) collective-permute-start(bf16[2,8,1,48,512]{4,3,2,1,0:T(8,128)(2,1)S(1)} %bitcast.49), channel_id=1, source_target_pairs={{0,1},{1,0},{2,3},{3,2},{4,5},{5,4},{6,7},{7,6},{8,9},{9,8},{10,11... | collective-permute-start | bytes 2359304 | tf_op jit(solution)/shard_map/ppermute | solution.py:87
  37.4 40.8 %copy-start = (bf16[1,8,2,48,512]{4,3,2,1,0:T(8,128)(2,1)}, bf16[1,8,2,48,512]{4,3,2,1,0:T(8,128)(2,1)S(1)}, u32[]{:S(2)}) copy-start(bf16[1,8,2,48,512]{4,3,2,1,0:T(8,128)(2,1)S(1)} %get-tuple-element.61) | copy-start | bytes 2359300
  38.3 6.9 %copy-start.10 = (bf16[48,896]{1,0:T(8,128)(2,1)S(1)}, bf16[48,896]{1,0:T(8,128)(2,1)}, u32[]{:S(2)}) copy-start(bf16[48,896]{1,0:T(8,128)(2,1)} %param.10) | copy-start | bytes 258052
  38.3 6.9 %copy-start.11 = (bf16[48,896]{1,0:T(8,128)(2,1)S(1)}, bf16[48,896]{1,0:T(8,128)(2,1)}, u32[]{:S(2)}) copy-start(bf16[48,896]{1,0:T(8,128)(2,1)} %param.9) | copy-start | bytes 258052
  40.4 27.9 %all-to-all-start.1 = ((bf16[4,192,896]{2,1,0:T(8,128)(2,1)}), bf16[4,192,896]{2,1,0:T(8,128)(2,1)S(1)}, u32[]{:S(2)}, u32[]{:S(2)}) async-start(bf16[4,192,896]{2,1,0:T(8,128)(2,1)} %bitcast.51), calls=%async_computation.1 | async-start | bytes 2752512 | tf_op jit(solution)/shard_map/all_to_all | solution.py:58
  68.3 24.6 %copy-start.6 = (bf16[256,896]{1,0:T(8,128)(2,1)S(1)}, bf16[256,896]{1,0:T(8,128)(2,1)}, u32[]{:S(2)}) copy-start(bf16[256,896]{1,0:T(8,128)(2,1)} %param.12) | copy-start | bytes 1376260
  69.3 23.6 %copy-start.7 = (bf16[256,896]{1,0:T(8,128)(2,1)S(1)}, bf16[256,896]{1,0:T(8,128)(2,1)}, u32[]{:S(2)}) copy-start(bf16[256,896]{1,0:T(8,128)(2,1)} %param.11) | copy-start | bytes 1376260
  69.3 15.2 %all-to-all-start.2 = ((bf16[4,48,896]{2,1,0:T(8,128)(2,1)}), bf16[4,48,896]{2,1,0:T(8,128)(2,1)S(1)}, u32[]{:S(2)}, u32[]{:S(2)}) async-start(bf16[4,48,896]{2,1,0:T(8,128)(2,1)} %bitcast.6), calls=%async_computation.2 | async-start | bytes 688128 | tf_op jit(solution)/shard_map/all_to_all | solution.py:58
  74.9 19.0 %collective-permute-start.3 = (bf16[192,1792]{1,0:T(8,128)(2,1)}, bf16[192,1792]{1,0:T(8,128)(2,1)}, u32[]{:S(2)}, u32[]{:S(2)}) collective-permute-start(bf16[192,1792]{1,0:T(8,128)(2,1)} %all_gather.3), channel_id=1, source_target_pairs={{0,384},{128,0},{256,128},{384,256},{1,385},{129,1},{257,129},{385... | collective-permute-start | bytes 2064392 | tf_op jit(solution)/shard_map/ppermute | solution.py:45
  85.3 13.7 %all-to-all-start.3 = ((bf16[4,48,896]{2,1,0:T(8,128)(2,1)}), bf16[4,48,896]{2,1,0:T(8,128)(2,1)S(1)}, u32[]{:S(2)}, u32[]{:S(2)}) async-start(bf16[4,48,896]{2,1,0:T(8,128)(2,1)} %broadcast_in_dim.37), calls=%async_computation.3 | async-start | bytes 688128 | tf_op jit(solution)/shard_map/all_to_all | solution.py:38
  88.9 21.3 %collective-permute-start.2 = (bf16[192,1792]{1,0:T(8,128)(2,1)}, bf16[192,1792]{1,0:T(8,128)(2,1)}, u32[]{:S(2)}, u32[]{:S(2)}) collective-permute-start(bf16[192,1792]{1,0:T(8,128)(2,1)} %all_gather.3), channel_id=1, source_target_pairs={{0,128},{128,256},{256,384},{384,0},{1,129},{129,257},{257,385},{3... | collective-permute-start | bytes 2064392 | tf_op jit(solution)/shard_map/ppermute | solution.py:44
  93.9 23.9 %collective-permute-start.4 = (bf16[192,1792]{1,0:T(8,128)(2,1)}, bf16[192,1792]{1,0:T(8,128)(2,1)}, u32[]{:S(2)}, u32[]{:S(2)}) collective-permute-start(bf16[192,1792]{1,0:T(8,128)(2,1)} %collective-permute-done.3), channel_id=1, source_target_pairs={{0,384},{128,0},{256,128},{384,256},{1,385},{129,1},{257,129},{385... | collective-permute-start | bytes 2064392 | tf_op jit(solution)/shard_map/ppermute | solution.py:46
  100.2 25.3 %all-to-all-start.4 = ((bf16[4,192,896]{2,1,0:T(8,128)(2,1)}), bf16[4,192,896]{2,1,0:T(8,128)(2,1)}, u32[]{:S(2)}, u32[]{:S(2)}) async-start(bf16[4,192,896]{2,1,0:T(8,128)(2,1)} %broadcast_in_dim.38), calls=%async_computation.4 | async-start | bytes 2752512 | tf_op jit(solution)/shard_map/all_to_all | solution.py:38
  106.9 31.6 %collective-permute-start.5 = (bf16[256,1792]{1,0:T(8,128)(2,1)}, bf16[256,1792]{1,0:T(8,128)(2,1)}, u32[]{:S(2)}, u32[]{:S(2)}) collective-permute-start(bf16[256,1792]{1,0:T(8,128)(2,1)} %pad_maximum_fusion.1), channel_id=1, source_target_pairs={{0,16},{16,0},{1,17},{17,1},{2,18},{18,2},{3,19},{19,3},{4,20},{20... | collective-permute-start | bytes 2752520 | tf_op jit(solution)/shard_map/ppermute | solution.py:20
  125.5 5.9 %copy-start.9 = (bf16[768,256]{1,0:T(8,128)(2,1)S(1)}, bf16[768,256]{1,0:T(8,128)(2,1)}, u32[]{:S(2)}) copy-start(bf16[768,256]{1,0:T(8,128)(2,1)} %slice.39) | copy-start | bytes 1179652
  125.5 31.1 %collective-permute-start.7 = (bf16[896,256]{1,0:T(8,128)(2,1)}, bf16[896,256]{1,0:T(8,128)(2,1)}, u32[]{:S(2)}, u32[]{:S(2)}) collective-permute-start(bf16[896,256]{1,0:T(8,128)(2,1)} %convolution_convert_fusion.2), channel_id=1, source_target_pairs={{0,16},{16,0},{1,17},{17,1},{2,18},{18,2},{3,19},{19,3},{4,20},{20... | collective-permute-start | bytes 1376264 | tf_op jit(solution)/shard_map/ppermute | solution.py:20
  133.5 5.0 %copy-start.2 = (bf16[768,1792]{1,0:T(8,128)(2,1)}, bf16[768,1792]{1,0:T(8,128)(2,1)S(1)}, u32[]{:S(2)}) copy-start(bf16[768,1792]{1,0:T(8,128)(2,1)S(1)} %pad_maximum_fusion) | copy-start | bytes 8257540
  133.5 25.5 %collective-permute-start.6 = (bf16[256,1792]{1,0:T(8,128)(2,1)}, bf16[256,1792]{1,0:T(8,128)(2,1)}, u32[]{:S(2)}, u32[]{:S(2)}) collective-permute-start(bf16[256,1792]{1,0:T(8,128)(2,1)} %convolution_convert_fusion), channel_id=1, source_target_pairs={{0,16},{16,0},{1,17},{17,1},{2,18},{18,2},{3,19},{19,3},{4,20},{20... | collective-permute-start | bytes 2752520 | tf_op jit(solution)/shard_map/ppermute | solution.py:20
  145.1 11.4 %copy-start.5 = (bf16[768,896]{1,0:T(8,128)(2,1)S(1)}, bf16[768,896]{1,0:T(8,128)(2,1)}, u32[]{:S(2)}) copy-start(bf16[768,896]{1,0:T(8,128)(2,1)} %copy-done.4) | copy-start | bytes 4128772
  146.1 21.1 %all-to-all-start.6 = ((bf16[16,48,256]{2,1,0:T(8,128)(2,1)}), bf16[16,48,256]{2,1,0:T(8,128)(2,1)S(1)}, u32[]{:S(2)}, u32[]{:S(2)}) async-start(bf16[16,48,256]{2,1,0:T(8,128)(2,1)} %bitcast.22), calls=%async_computation.6 | async-start | bytes 786432 | tf_op jit(solution)/shard_map/all_to_all | solution.py:136
  154.3 4.6 %copy-start.3 = (bf16[768,1792]{1,0:T(8,128)(2,1)S(1)}, bf16[768,1792]{1,0:T(8,128)(2,1)}, u32[]{:S(2)}) copy-start(bf16[768,1792]{1,0:T(8,128)(2,1)} %copy-done.2) | copy-start | bytes 8257540
  154.3 4.6 %copy-start.8 = (bf16[768,256]{1,0:T(8,128)(2,1)S(1)}, bf16[768,256]{1,0:T(8,128)(2,1)}, u32[]{:S(2)}) copy-start(bf16[768,256]{1,0:T(8,128)(2,1)} %slice.38) | copy-start | bytes 1179652
  (3 other events, 5.3 us)

commit v4 on v3

--- a/solution.py
+++ b/solution.py
@@ -103,9 +103,12 @@
     both_w = jnp.concatenate([gate_weight, up_weight], axis=1)
     part, own, other = tie(part, own, other)
     hidden_grad = spread(part, "zq", 4)
-    hidden_grad, both_w, pre = tie(hidden_grad, both_w, pre)
+    hidden_grad, both_w, pre, gate_weight, up_weight = tie(
+        hidden_grad, both_w, pre, gate_weight, up_weight
+    )
     hidden_grad = spread(hidden_grad, "x", 4)
     both_w_other = swap(both_w)
+    both_w = jnp.concatenate([gate_weight, up_weight], axis=1)
 
     pre = assemble(pre, pre_pieces, "x")
     gate_val = pre[:, :units].astype(F32)
@@ -114,7 +117,7 @@
     silu = gate_val * sigma
     hidden = (silu * up_val).astype(BF)
     down_other = contract_rows(hidden, grads[:, width:]).astype(BF)
-    hidden_grad, down_other, pre = tie(hidden_grad, down_other, pre)
+    hidden_grad, down_other, pre, both_w = tie(hidden_grad, down_other, pre, both_w)
     down_other = swap(down_other)
 
     gate_val = pre[:, :units].astype(F32)

time: 169 us -> 168 us (level)
  no operation moved by 1% of the time
where the time goes in v4:
time: 168 us; the launch traced here: 167 us
  starting transfers between devices  59.4 us (35%)
  waiting for transfers between devices  42.4 us (25%)
  blocking collectives  27.3 us (16%)
  matrix products  15.5 us (9%)
  local copies, waits for them, and re-layouts  11.5 us (7%)
  other arithmetic  9.69 us (6%)
    all_gather x1, blocking collectives, body(): pre = lax.all_gather(pre, 'zq', axis=0, tiled=True)  23 us
    ppermute x4, waiting for transfers between devices, swap(): return lax.ppermute(value, 'zw', SWAP)  17.8 us
    ppermute x4, starting transfers between devices, swap(): return lax.ppermute(value, 'zw', SWAP)  11.6 us
    all_to_all x2, starting transfers between devices, scatter_sum(): return lax.all_to_all(value, axis, 0, 0, tiled=True).astype(F32).sum(axis=0)  10.6 us
    dot_general x5, matrix products, contract_rows(): lax.dot_general(left, right, (((0,), (0,)), ((), ())), preferred_element_...  10.4 us
    all_to_all x2, starting transfers between devices, spread(): lax.all_to_all(copies, axis, 0, 0, tiled=True)  9.57 us
    all_to_all x1, starting transfers between devices, body(): rows = lax.all_to_all(rows, ('zw', 'y'), 0, 0, tiled=True)  9.37 us
    all_to_all x1, starting transfers between devices, body(): term = lax.all_to_all(term, ('zw', 'y'), 0, 0, tiled=True)  7.95 us
  transfers between devices with their start and end apart: 14, of which 7 were waited for; matrix products, arithmetic and copies ran while one was open for 17% of the time, Pallas kernels for 0%

profile of v4, /device:TPU:14, one launch (start us, length us, event | category | flops | bytes accessed | tf_op | source)
XLA Modules:
  0.0 166.8 jit_solution(154189623657200577)
XLA Ops:
  2.4 9.4 %all-to-all-start = ((bf16[16,48,512]{2,1,0:T(8,128)(2,1)}), bf16[16,48,512]{2,1,0:T(8,128)(2,1)S(1)}, u32[]{:S(2)}, u32[]{:S(2)}) async-start(bf16[16,48,512]{2,1,0:T(8,128)(2,1)} %bitcast.1), calls=%async_computation | async-start | bytes 1572864 | tf_op jit(solution)/shard_map/all_to_all | solution.py:82
  11.8 3.4 %collective-permute-start = (bf16[896,256]{1,0:T(8,128)(2,1)}, bf16[896,256]{1,0:T(8,128)(2,1)S(1)}, u32[]{:S(2)}, u32[]{:S(2)}) collective-permute-start(bf16[896,256]{1,0:T(8,128)(2,1)} %param.13), channel_id=1, source_target_pairs={{0,16},{16,0},{1,17},{17,1},{2,18},{18,2},{3,19},{19,3},{4,20},{20... | collective-permute-start | bytes 1376264 | tf_op jit(solution)/shard_map/ppermute | solution.py:20
  15.2 17.8 %collective-permute-done = bf16[896,256]{1,0:T(8,128)(2,1)S(1)} collective-permute-done((bf16[896,256]{1,0:T(8,128)(2,1)}, bf16[896,256]{1,0:T(8,128)(2,1)S(1)}, u32[]{:S(2)}, u32[]{:S(2)}) %collective-permute-start) | collective-permute-done | bytes 458784 | tf_op jit(solution)/shard_map/ppermute | solution.py:20
  34.9 2.2 %collective-permute-done.1 = bf16[2,8,1,48,512]{4,3,2,1,0:T(8,128)(2,1)S(1)} collective-permute-done((bf16[2,8,1,48,512]{4,3,2,1,0:T(8,128)(2,1)S(1)}, bf16[2,8,1,48,512]{4,3,2,1,0:T(8,128)(2,1)S(1)}, u32[]{:S(2)}, u32[]{:S(2)}) %collective-permute-start.1) | collective-permute-done | bytes 786464 | tf_op jit(solution)/shard_map/ppermute | solution.py:87
  40.5 4.8 %all-to-all-start.1 = ((bf16[4,192,896]{2,1,0:T(8,128)(2,1)}), bf16[4,192,896]{2,1,0:T(8,128)(2,1)S(1)}, u32[]{:S(2)}, u32[]{:S(2)}) async-start(bf16[4,192,896]{2,1,0:T(8,128)(2,1)} %bitcast.51), calls=%async_computation.1 | async-start | bytes 2752512 | tf_op jit(solution)/shard_map/all_to_all | solution.py:58
  45.2 23.0 %all_gather.3 = bf16[192,1792]{1,0:T(8,128)(2,1)} all-gather(bf16[48,1792]{1,0:T(8,128)(2,1)S(1)} %pad_maximum_fusion.3), channel_id=1, replica_groups=mesh['x'=4,'zq'=4,'zw'=2,'y'=8,'core'=2] {'zq'}, dimensions={0}, use_global_device_ids=true | all-gather | bytes 860160 | tf_op jit(solution)/shard_map/all_gather | solution.py:97
  69.2 5.8 %all-to-all-start.2 = ((bf16[4,48,896]{2,1,0:T(8,128)(2,1)}), bf16[4,48,896]{2,1,0:T(8,128)(2,1)S(1)}, u32[]{:S(2)}, u32[]{:S(2)}) async-start(bf16[4,48,896]{2,1,0:T(8,128)(2,1)} %bitcast.53), calls=%async_computation.2 | async-start | bytes 688128 | tf_op jit(solution)/shard_map/all_to_all | solution.py:58
  75.0 2.6 %collective-permute-start.3 = (bf16[192,1792]{1,0:T(8,128)(2,1)}, bf16[192,1792]{1,0:T(8,128)(2,1)}, u32[]{:S(2)}, u32[]{:S(2)}) collective-permute-start(bf16[192,1792]{1,0:T(8,128)(2,1)} %all_gather.3), channel_id=1, source_target_pairs={{0,384},{128,0},{256,128},{384,256},{1,385},{129,1},{257,129},{385... | collective-permute-start | bytes 2064392 | tf_op jit(solution)/shard_map/ppermute | solution.py:45
  79.2 5.5 %all-to-all-done.2 = bf16[4,48,896]{2,1,0:T(8,128)(2,1)S(1)} async-done(((bf16[4,48,896]{2,1,0:T(8,128)(2,1)}), bf16[4,48,896]{2,1,0:T(8,128)(2,1)S(1)}, u32[]{:S(2)}, u32[]{:S(2)}) %all-to-all-start.2) | async-done | bytes 344096 | tf_op jit(solution)/shard_map/all_to_all | solution.py:58
  85.5 3.5 %all-to-all-start.3 = ((bf16[4,48,896]{2,1,0:T(8,128)(2,1)}), bf16[4,48,896]{2,1,0:T(8,128)(2,1)S(1)}, u32[]{:S(2)}, u32[]{:S(2)}) async-start(bf16[4,48,896]{2,1,0:T(8,128)(2,1)} %broadcast_in_dim.37), calls=%async_computation.3 | async-start | bytes 688128 | tf_op jit(solution)/shard_map/all_to_all | solution.py:38
  89.0 3.9 %collective-permute-start.2 = (bf16[192,1792]{1,0:T(8,128)(2,1)}, bf16[192,1792]{1,0:T(8,128)(2,1)}, u32[]{:S(2)}, u32[]{:S(2)}) collective-permute-start(bf16[192,1792]{1,0:T(8,128)(2,1)} %all_gather.3), channel_id=1, source_target_pairs={{0,128},{128,256},{256,384},{384,0},{1,129},{129,257},{257,385},{3... | collective-permute-start | bytes 2064392 | tf_op jit(solution)/shard_map/ppermute | solution.py:44
  95.9 3.2 %all-to-all-done.3 = bf16[4,48,896]{2,1,0:T(8,128)(2,1)S(1)} async-done(((bf16[4,48,896]{2,1,0:T(8,128)(2,1)}), bf16[4,48,896]{2,1,0:T(8,128)(2,1)S(1)}, u32[]{:S(2)}, u32[]{:S(2)}) %all-to-all-start.3) | async-done | bytes 344096 | tf_op jit(solution)/shard_map/all_to_all | solution.py:38
  100.3 6.1 %all-to-all-start.4 = ((bf16[4,192,896]{2,1,0:T(8,128)(2,1)}), bf16[4,192,896]{2,1,0:T(8,128)(2,1)}, u32[]{:S(2)}, u32[]{:S(2)}) async-start(bf16[4,192,896]{2,1,0:T(8,128)(2,1)} %broadcast_in_dim.38), calls=%async_computation.4 | async-start | bytes 2752512 | tf_op jit(solution)/shard_map/all_to_all | solution.py:38
  106.4 2.2 %collective-permute-start.5 = (bf16[256,1792]{1,0:T(8,128)(2,1)}, bf16[256,1792]{1,0:T(8,128)(2,1)}, u32[]{:S(2)}, u32[]{:S(2)}) collective-permute-start(bf16[256,1792]{1,0:T(8,128)(2,1)} %pad_maximum_fusion.1), channel_id=1, source_target_pairs={{0,16},{16,0},{1,17},{17,1},{2,18},{18,2},{3,19},{19,3},{4,20},{20... | collective-permute-start | bytes 2752520 | tf_op jit(solution)/shard_map/ppermute | solution.py:20
  112.1 5.1 %collective-permute-done.4 = bf16[192,1792]{1,0:T(8,128)(2,1)} collective-permute-done((bf16[192,1792]{1,0:T(8,128)(2,1)}, bf16[192,1792]{1,0:T(8,128)(2,1)}, u32[]{:S(2)}, u32[]{:S(2)}) %collective-permute-start.4) | collective-permute-done | bytes 688160 | tf_op jit(solution)/shard_map/ppermute | solution.py:46
  122.9 2.8 %all-to-all-done.4 = bf16[4,192,896]{2,1,0:T(8,128)(2,1)} async-done(((bf16[4,192,896]{2,1,0:T(8,128)(2,1)}), bf16[4,192,896]{2,1,0:T(8,128)(2,1)}, u32[]{:S(2)}, u32[]{:S(2)}) %all-to-all-start.4) | async-done | bytes 1376288 | tf_op jit(solution)/shard_map/all_to_all | solution.py:38
  125.7 2.2 %collective-permute-start.7 = (bf16[896,256]{1,0:T(8,128)(2,1)}, bf16[896,256]{1,0:T(8,128)(2,1)}, u32[]{:S(2)}, u32[]{:S(2)}) collective-permute-start(bf16[896,256]{1,0:T(8,128)(2,1)} %convolution_convert_fusion.2), channel_id=1, source_target_pairs={{0,16},{16,0},{1,17},{17,1},{2,18},{18,2},{3,19},{19,3},{4,20},{20... | collective-permute-start | bytes 1376264 | tf_op jit(solution)/shard_map/ppermute | solution.py:20
  127.9 2.8 %fusion.6 = (bf16[768,896]{1,0:T(8,128)(2,1)S(1)}, bf16[768,896]{1,0:T(8,128)(2,1)S(1)}) fusion(bf16[768,896]{1,0:T(8,128)(2,1)} %bitcast.8, bf16[768,1792]{1,0:T(8,128)(2,1)S(1)} %bitcast.42), kind=kLoop, calls=%fused_computation.13 | loop fusion | flops 11010048 | bytes 6881280 | tf_op jit(solution)/shard_map/convert_element_type | solution.py:130
  132.8 3.9 %collective-permute-start.6 = (bf16[256,1792]{1,0:T(8,128)(2,1)}, bf16[256,1792]{1,0:T(8,128)(2,1)}, u32[]{:S(2)}, u32[]{:S(2)}) collective-permute-start(bf16[256,1792]{1,0:T(8,128)(2,1)} %convolution_convert_fusion), channel_id=1, source_target_pairs={{0,16},{16,0},{1,17},{17,1},{2,18},{18,2},{3,19},{19,3},{4,20},{20... | collective-permute-start | bytes 2752520 | tf_op jit(solution)/shard_map/ppermute | solution.py:20
  139.9 4.4 %all_to_all.35 = bf16[2,2,8,48,256]{4,3,2,1,0:T(8,128)(2,1)S(1)} all-to-all(bf16[2,2,8,48,256]{4,3,2,1,0:T(8,128)(2,1)S(1)} %maximum_select_fusion.1), channel_id=1, replica_groups=mesh['x'=4,'zq'=4,'zw'=2,'y'=8,'core'=2] {'core'}, dimensions={0} | all-to-all | bytes 1572864 | tf_op jit(solution)/shard_map/all_to_all | solution.py:137
  145.3 7.9 %all-to-all-start.6 = ((bf16[16,48,256]{2,1,0:T(8,128)(2,1)}), bf16[16,48,256]{2,1,0:T(8,128)(2,1)S(1)}, u32[]{:S(2)}, u32[]{:S(2)}) async-start(bf16[16,48,256]{2,1,0:T(8,128)(2,1)} %bitcast.22), calls=%async_computation.6 | async-start | bytes 786432 | tf_op jit(solution)/shard_map/all_to_all | solution.py:139
  155.3 2.4 %add_convert_fusion = bf16[896,256]{1,0:T(8,128)(2,1)} fusion(bf16[896,256]{1,0:T(8,128)(2,1)} %collective-permute-done.7, bf16[768,896]{1,0:T(8,128)(2,1)S(1)} %copy-done.9, bf16[768,512]{1,0:T(8,128)(2,1)S(1)} %bitcast.45), kind=kOutput, calls=%fused_computation.36 | convolution fusion | flops 353009664 | bytes 2686976 | tf_op jit(solution)/shard_map/dot_general | solution.py:12
  157.7 2.7 %add_convert_fusion.1 = (bf16[256,896]{1,0:T(8,128)(2,1)}, bf16[256,896]{1,0:T(8,128)(2,1)}) fusion(bf16[256,1792]{1,0:T(8,128)(2,1)} %collective-permute-done.6, f32[256,896]{1,0:T(8,128)S(1)} %fusion.15, bf16[768,256]{1,0:T(8,128)(2,1)S(1)} %copy-done.11, bf16[768,1792]{1,0:T(8,128)(2,1)S(1)} %copy-done.3), kind=kOutput, calls=%fused_computation.37 | convolution fusion | flops 353697792 | bytes 4521984 | tf_op jit(solution)/shard_map/dot_general | solution.py:12
  160.4 5.7 %all-to-all-done.6 = bf16[16,48,256]{2,1,0:T(8,128)(2,1)S(1)} async-done(((bf16[16,48,256]{2,1,0:T(8,128)(2,1)}), bf16[16,48,256]{2,1,0:T(8,128)(2,1)S(1)}, u32[]{:S(2)}, u32[]{:S(2)}) %all-to-all-start.6) | async-done | bytes 393248 | tf_op jit(solution)/shard_map/all_to_all | solution.py:139
  (73 shorter events, 32.7 us)
Async XLA Ops:
  2.4 30.5 %all-to-all-start = ((bf16[16,48,512]{2,1,0:T(8,128)(2,1)}), bf16[16,48,512]{2,1,0:T(8,128)(2,1)S(1)}, u32[]{:S(2)}, u32[]{:S(2)}) async-start(bf16[16,48,512]{2,1,0:T(8,128)(2,1)} %bitcast.1), calls=%async_computation | async-start | bytes 1572864 | tf_op jit(solution)/shard_map/all_to_all | solution.py:82
  11.8 21.2 %collective-permute-start = (bf16[896,256]{1,0:T(8,128)(2,1)}, bf16[896,256]{1,0:T(8,128)(2,1)S(1)}, u32[]{:S(2)}, u32[]{:S(2)}) collective-permute-start(bf16[896,256]{1,0:T(8,128)(2,1)} %param.13), channel_id=1, source_target_pairs={{0,16},{16,0},{1,17},{17,1},{2,18},{18,2},{3,19},{19,3},{4,20},{20... | collective-permute-start | bytes 1376264 | tf_op jit(solution)/shard_map/ppermute | solution.py:20
  33.0 4.2 %collective-permute-start.1 = (bf16[2,8,1,48,512]{4,3,2,1,0:T(8,128)(2,1)S(1)}, bf16[2,8,1,48,512]{4,3,2,1,0:T(8,128)(2,1)S(1)}, u32[]{:S(2)}, u32[]{:S(2)}) collective-permute-start(bf16[2,8,1,48,512]{4,3,2,1,0:T(8,128)(2,1)S(1)} %bitcast.49), channel_id=1, source_target_pairs={{0,1},{1,0},{2,3},{3,2},{4,5},{5,4},{6,7},{7,6},{8,9},{9,8},{10,11... | collective-permute-start | bytes 2359304 | tf_op jit(solution)/shard_map/ppermute | solution.py:87
  37.5 40.9 %copy-start = (bf16[1,8,2,48,512]{4,3,2,1,0:T(8,128)(2,1)}, bf16[1,8,2,48,512]{4,3,2,1,0:T(8,128)(2,1)S(1)}, u32[]{:S(2)}) copy-start(bf16[1,8,2,48,512]{4,3,2,1,0:T(8,128)(2,1)S(1)} %get-tuple-element.67) | copy-start | bytes 2359300
  38.3 6.9 %copy-start.13 = (bf16[48,896]{1,0:T(8,128)(2,1)S(1)}, bf16[48,896]{1,0:T(8,128)(2,1)}, u32[]{:S(2)}) copy-start(bf16[48,896]{1,0:T(8,128)(2,1)} %param.10) | copy-start | bytes 258052
  38.3 6.9 %copy-start.14 = (bf16[48,896]{1,0:T(8,128)(2,1)S(1)}, bf16[48,896]{1,0:T(8,128)(2,1)}, u32[]{:S(2)}) copy-start(bf16[48,896]{1,0:T(8,128)(2,1)} %param.9) | copy-start | bytes 258052
  40.5 27.8 %all-to-all-start.1 = ((bf16[4,192,896]{2,1,0:T(8,128)(2,1)}), bf16[4,192,896]{2,1,0:T(8,128)(2,1)S(1)}, u32[]{:S(2)}, u32[]{:S(2)}) async-start(bf16[4,192,896]{2,1,0:T(8,128)(2,1)} %bitcast.51), calls=%async_computation.1 | async-start | bytes 2752512 | tf_op jit(solution)/shard_map/all_to_all | solution.py:58
  68.2 24.7 %copy-start.4 = (bf16[256,896]{1,0:T(8,128)(2,1)S(1)}, bf16[256,896]{1,0:T(8,128)(2,1)}, u32[]{:S(2)}) copy-start(bf16[256,896]{1,0:T(8,128)(2,1)} %param.12) | copy-start | bytes 1376260
  69.2 23.7 %copy-start.6 = (bf16[256,896]{1,0:T(8,128)(2,1)S(1)}, bf16[256,896]{1,0:T(8,128)(2,1)}, u32[]{:S(2)}) copy-start(bf16[256,896]{1,0:T(8,128)(2,1)} %param.11) | copy-start | bytes 1376260
  69.2 15.5 %all-to-all-start.2 = ((bf16[4,48,896]{2,1,0:T(8,128)(2,1)}), bf16[4,48,896]{2,1,0:T(8,128)(2,1)S(1)}, u32[]{:S(2)}, u32[]{:S(2)}) async-start(bf16[4,48,896]{2,1,0:T(8,128)(2,1)} %bitcast.53), calls=%async_computation.2 | async-start | bytes 688128 | tf_op jit(solution)/shard_map/all_to_all | solution.py:58
  75.0 18.9 %collective-permute-start.3 = (bf16[192,1792]{1,0:T(8,128)(2,1)}, bf16[192,1792]{1,0:T(8,128)(2,1)}, u32[]{:S(2)}, u32[]{:S(2)}) collective-permute-start(bf16[192,1792]{1,0:T(8,128)(2,1)} %all_gather.3), channel_id=1, source_target_pairs={{0,384},{128,0},{256,128},{384,256},{1,385},{129,1},{257,129},{385... | collective-permute-start | bytes 2064392 | tf_op jit(solution)/shard_map/ppermute | solution.py:45
  85.5 13.6 %all-to-all-start.3 = ((bf16[4,48,896]{2,1,0:T(8,128)(2,1)}), bf16[4,48,896]{2,1,0:T(8,128)(2,1)S(1)}, u32[]{:S(2)}, u32[]{:S(2)}) async-start(bf16[4,48,896]{2,1,0:T(8,128)(2,1)} %broadcast_in_dim.37), calls=%async_computation.3 | async-start | bytes 688128 | tf_op jit(solution)/shard_map/all_to_all | solution.py:38
  89.0 21.9 %collective-permute-start.2 = (bf16[192,1792]{1,0:T(8,128)(2,1)}, bf16[192,1792]{1,0:T(8,128)(2,1)}, u32[]{:S(2)}, u32[]{:S(2)}) collective-permute-start(bf16[192,1792]{1,0:T(8,128)(2,1)} %all_gather.3), channel_id=1, source_target_pairs={{0,128},{128,256},{256,384},{384,0},{1,129},{129,257},{257,385},{3... | collective-permute-start | bytes 2064392 | tf_op jit(solution)/shard_map/ppermute | solution.py:44
  93.9 23.3 %collective-permute-start.4 = (bf16[192,1792]{1,0:T(8,128)(2,1)}, bf16[192,1792]{1,0:T(8,128)(2,1)}, u32[]{:S(2)}, u32[]{:S(2)}) collective-permute-start(bf16[192,1792]{1,0:T(8,128)(2,1)} %collective-permute-done.3), channel_id=1, source_target_pairs={{0,384},{128,0},{256,128},{384,256},{1,385},{129,1},{257,129},{385... | collective-permute-start | bytes 2064392 | tf_op jit(solution)/shard_map/ppermute | solution.py:46
  100.3 25.4 %all-to-all-start.4 = ((bf16[4,192,896]{2,1,0:T(8,128)(2,1)}), bf16[4,192,896]{2,1,0:T(8,128)(2,1)}, u32[]{:S(2)}, u32[]{:S(2)}) async-start(bf16[4,192,896]{2,1,0:T(8,128)(2,1)} %broadcast_in_dim.38), calls=%async_computation.4 | async-start | bytes 2752512 | tf_op jit(solution)/shard_map/all_to_all | solution.py:38
  106.4 31.3 %collective-permute-start.5 = (bf16[256,1792]{1,0:T(8,128)(2,1)}, bf16[256,1792]{1,0:T(8,128)(2,1)}, u32[]{:S(2)}, u32[]{:S(2)}) collective-permute-start(bf16[256,1792]{1,0:T(8,128)(2,1)} %pad_maximum_fusion.1), channel_id=1, source_target_pairs={{0,16},{16,0},{1,17},{17,1},{2,18},{18,2},{3,19},{19,3},{4,20},{20... | collective-permute-start | bytes 2752520 | tf_op jit(solution)/shard_map/ppermute | solution.py:20
  125.7 5.1 %copy-start.12 = (bf16[768,256]{1,0:T(8,128)(2,1)S(1)}, bf16[768,256]{1,0:T(8,128)(2,1)}, u32[]{:S(2)}) copy-start(bf16[768,256]{1,0:T(8,128)(2,1)} %slice.39) | copy-start | bytes 1179652
  125.7 29.6 %collective-permute-start.7 = (bf16[896,256]{1,0:T(8,128)(2,1)}, bf16[896,256]{1,0:T(8,128)(2,1)}, u32[]{:S(2)}, u32[]{:S(2)}) collective-permute-start(bf16[896,256]{1,0:T(8,128)(2,1)} %convolution_convert_fusion.2), channel_id=1, source_target_pairs={{0,16},{16,0},{1,17},{17,1},{2,18},{18,2},{3,19},{19,3},{4,20},{20... | collective-permute-start | bytes 1376264 | tf_op jit(solution)/shard_map/ppermute | solution.py:20
  132.8 4.8 %copy-start.2 = (bf16[768,1792]{1,0:T(8,128)(2,1)}, bf16[768,1792]{1,0:T(8,128)(2,1)S(1)}, u32[]{:S(2)}) copy-start(bf16[768,1792]{1,0:T(8,128)(2,1)S(1)} %pad_maximum_fusion) | copy-start | bytes 8257540
  132.8 24.9 %collective-permute-start.6 = (bf16[256,1792]{1,0:T(8,128)(2,1)}, bf16[256,1792]{1,0:T(8,128)(2,1)}, u32[]{:S(2)}, u32[]{:S(2)}) collective-permute-start(bf16[256,1792]{1,0:T(8,128)(2,1)} %convolution_convert_fusion), channel_id=1, source_target_pairs={{0,16},{16,0},{1,17},{17,1},{2,18},{18,2},{3,19},{19,3},{4,20},{20... | collective-permute-start | bytes 2752520 | tf_op jit(solution)/shard_map/ppermute | solution.py:20
  139.8 13.4 %copy-start.11 = (bf16[768,256]{1,0:T(8,128)(2,1)S(1)}, bf16[768,256]{1,0:T(8,128)(2,1)}, u32[]{:S(2)}) copy-start(bf16[768,256]{1,0:T(8,128)(2,1)} %slice.38) | copy-start | bytes 1179652
  144.3 11.0 %copy-start.9 = (bf16[768,896]{1,0:T(8,128)(2,1)S(1)}, bf16[768,896]{1,0:T(8,128)(2,1)}, u32[]{:S(2)}) copy-start(bf16[768,896]{1,0:T(8,128)(2,1)} %copy-done.8) | copy-start | bytes 4128772
  145.3 20.8 %all-to-all-start.6 = ((bf16[16,48,256]{2,1,0:T(8,128)(2,1)}), bf16[16,48,256]{2,1,0:T(8,128)(2,1)S(1)}, u32[]{:S(2)}, u32[]{:S(2)}) async-start(bf16[16,48,256]{2,1,0:T(8,128)(2,1)} %bitcast.22), calls=%async_computation.6 | async-start | bytes 786432 | tf_op jit(solution)/shard_map/all_to_all | solution.py:139
  153.2 4.5 %copy-start.3 = (bf16[768,1792]{1,0:T(8,128)(2,1)S(1)}, bf16[768,1792]{1,0:T(8,128)(2,1)}, u32[]{:S(2)}) copy-start(bf16[768,1792]{1,0:T(8,128)(2,1)} %copy-done.2) | copy-start | bytes 8257540
  (6 other events, 16.4 us)

commit v5 on v4

--- a/solution.py
+++ b/solution.py
@@ -116,18 +116,17 @@
     sigma = jax.nn.sigmoid(gate_val)
     silu = gate_val * sigma
     hidden = (silu * up_val).astype(BF)
+    gate_scale = (up_val * sigma * (1.0 + gate_val * (1.0 - sigma))).astype(BF)
+    up_scale = silu.astype(BF)
     down_other = contract_rows(hidden, grads[:, width:]).astype(BF)
-    hidden_grad, down_other, pre, both_w = tie(hidden_grad, down_other, pre, both_w)
+    hidden_grad, down_other, gate_scale, up_scale, both_w = tie(
+        hidden_grad, down_other, gate_scale, up_scale, both_w
+    )
     down_other = swap(down_other)
-
-    gate_val = pre[:, :units].astype(F32)
-    up_val = pre[:, units:].astype(F32)
-    sigma = jax.nn.sigmoid(gate_val)
-    silu = gate_val * sigma
     hidden_grad = hidden_grad.astype(F32)
-    gate_delta = hidden_grad * up_val * sigma * (1.0 + gate_val * (1.0 - sigma))
-    up_delta = hidden_grad * silu
-    both = jnp.concatenate([gate_delta.astype(BF), up_delta.astype(BF)], axis=1)
+    gate_delta = (hidden_grad * gate_scale.astype(F32)).astype(BF)
+    up_delta = (hidden_grad * up_scale.astype(F32)).astype(BF)
+    both = jnp.concatenate([gate_delta, up_delta], axis=1)
     sums_other = contract_rows(other, both).astype(BF)
     both, sums_other = tie(both, sums_other)
     sums_other = swap(sums_other)

time: 168 us -> 168 us (level)
  other arithmetic: 9.69 us -> 11.7 us
    all_to_all x2, waiting for transfers between devices: 5.98 us -> 4.02 us  [spread(): lax.all_to_all(copies, axis, 0, 0, tiled=True)]
  transfers between devices with their start and end apart: 14 -> 14, of which waited for: 7 -> 7; matrix products, arithmetic and copies ran while one was open for 17% -> 18% of each run, Pallas kernels for 0% -> 0%
where the time goes in v5:
time: 168 us; the launch traced here: 167 us
  starting transfers between devices  58.9 us (35%)
  waiting for transfers between devices  41.9 us (25%)
  blocking collectives  27.4 us (16%)
  matrix products  15.5 us (9%)
  other arithmetic  11.7 us (7%)
  local copies, waits for them, and re-layouts  10.3 us (6%)
    all_gather x1, blocking collectives, body(): pre = lax.all_gather(pre, 'zq', axis=0, tiled=True)  23 us
    ppermute x4, waiting for transfers between devices, swap(): return lax.ppermute(value, 'zw', SWAP)  17.8 us
    ppermute x4, starting transfers between devices, swap(): return lax.ppermute(value, 'zw', SWAP)  12.1 us
    all_to_all x2, starting transfers between devices, scatter_sum(): return lax.all_to_all(value, axis, 0, 0, tiled=True).astype(F32).sum(axis=0)  10.5 us
    dot_general x5, matrix products, contract_rows(): lax.dot_general(left, right, (((0,), (0,)), ((), ())), preferred_element_...  10.3 us
    all_to_all x1, starting transfers between devices, body(): rows = lax.all_to_all(rows, ('zw', 'y'), 0, 0, tiled=True)  9.37 us
    all_to_all x2, starting transfers between devices, spread(): lax.all_to_all(copies, axis, 0, 0, tiled=True)  8.82 us
    all_to_all x1, starting transfers between devices, body(): term = lax.all_to_all(term, ('zw', 'y'), 0, 0, tiled=True)  7.78 us
  transfers between devices with their start and end apart: 14, of which 7 were waited for; matrix products, arithmetic and copies ran while one was open for 18% of the time, Pallas kernels for 0%

profile of v5, /device:TPU:14, one launch (start us, length us, event | category | flops | bytes accessed | tf_op | source)
XLA Modules:
  0.0 166.7 jit_solution(8926493105780909251)
XLA Ops:
  2.4 9.4 %all-to-all-start = ((bf16[16,48,512]{2,1,0:T(8,128)(2,1)}), bf16[16,48,512]{2,1,0:T(8,128)(2,1)S(1)}, u32[]{:S(2)}, u32[]{:S(2)}) async-start(bf16[16,48,512]{2,1,0:T(8,128)(2,1)} %bitcast.1), calls=%async_computation | async-start | bytes 1572864 | tf_op jit(solution)/shard_map/all_to_all | solution.py:82
  11.8 3.4 %collective-permute-start = (bf16[896,256]{1,0:T(8,128)(2,1)}, bf16[896,256]{1,0:T(8,128)(2,1)S(1)}, u32[]{:S(2)}, u32[]{:S(2)}) collective-permute-start(bf16[896,256]{1,0:T(8,128)(2,1)} %param.13), channel_id=1, source_target_pairs={{0,16},{16,0},{1,17},{17,1},{2,18},{18,2},{3,19},{19,3},{4,20},{20... | collective-permute-start | bytes 1376264 | tf_op jit(solution)/shard_map/ppermute | solution.py:20
  15.2 17.8 %collective-permute-done = bf16[896,256]{1,0:T(8,128)(2,1)S(1)} collective-permute-done((bf16[896,256]{1,0:T(8,128)(2,1)}, bf16[896,256]{1,0:T(8,128)(2,1)S(1)}, u32[]{:S(2)}, u32[]{:S(2)}) %collective-permute-start) | collective-permute-done | bytes 458784 | tf_op jit(solution)/shard_map/ppermute | solution.py:20
  34.9 2.2 %collective-permute-done.1 = bf16[2,8,1,48,512]{4,3,2,1,0:T(8,128)(2,1)S(1)} collective-permute-done((bf16[2,8,1,48,512]{4,3,2,1,0:T(8,128)(2,1)S(1)}, bf16[2,8,1,48,512]{4,3,2,1,0:T(8,128)(2,1)S(1)}, u32[]{:S(2)}, u32[]{:S(2)}) %collective-permute-start.1) | collective-permute-done | bytes 786464 | tf_op jit(solution)/shard_map/ppermute | solution.py:87
  38.3 2.1 %convolution_convert_fusion.1 = bf16[768,896]{1,0:T(8,128)(2,1)} fusion(bf16[896,256]{1,0:T(8,128)(2,1)S(1)} %collective-permute-done, bf16[896,256]{1,0:T(8,128)(2,1)S(1)} %copy-done.15, bf16[768,256]{1,0:T(8,128)(2,1)S(1)} %slice.41, bf16[768,256]{1,0:T(8,128)(2,1)S(1)} %slice.40), kind=kOutput, calls=%fused_computation.18 | convolution fusion | flops 708739072 | bytes 3080192 | tf_op jit(solution)/shard_map/dot_general | solution.py:16
  40.4 4.8 %all-to-all-start.1 = ((bf16[4,192,896]{2,1,0:T(8,128)(2,1)}), bf16[4,192,896]{2,1,0:T(8,128)(2,1)S(1)}, u32[]{:S(2)}, u32[]{:S(2)}) async-start(bf16[4,192,896]{2,1,0:T(8,128)(2,1)} %bitcast.51), calls=%async_computation.1 | async-start | bytes 2752512 | tf_op jit(solution)/shard_map/all_to_all | solution.py:58
  45.2 23.0 %all_gather.3 = bf16[192,1792]{1,0:T(8,128)(2,1)} all-gather(bf16[48,1792]{1,0:T(8,128)(2,1)S(1)} %pad_maximum_fusion.3), channel_id=1, replica_groups=mesh['x'=4,'zq'=4,'zw'=2,'y'=8,'core'=2] {'zq'}, dimensions={0}, use_global_device_ids=true | all-gather | bytes 860160 | tf_op jit(solution)/shard_map/all_gather | solution.py:97
  69.2 5.7 %all-to-all-start.2 = ((bf16[4,48,896]{2,1,0:T(8,128)(2,1)}), bf16[4,48,896]{2,1,0:T(8,128)(2,1)}, u32[]{:S(2)}, u32[]{:S(2)}) async-start(bf16[4,48,896]{2,1,0:T(8,128)(2,1)} %bitcast.53), calls=%async_computation.2 | async-start | bytes 688128 | tf_op jit(solution)/shard_map/all_to_all | solution.py:58
  75.0 2.7 %collective-permute-start.3 = (bf16[192,1792]{1,0:T(8,128)(2,1)}, bf16[192,1792]{1,0:T(8,128)(2,1)}, u32[]{:S(2)}, u32[]{:S(2)}) collective-permute-start(bf16[192,1792]{1,0:T(8,128)(2,1)} %all_gather.3), channel_id=1, source_target_pairs={{0,384},{128,0},{256,128},{384,256},{1,385},{129,1},{257,129},{385... | collective-permute-start | bytes 2064392 | tf_op jit(solution)/shard_map/ppermute | solution.py:45
  79.2 5.7 %all-to-all-done.2 = bf16[4,48,896]{2,1,0:T(8,128)(2,1)} async-done(((bf16[4,48,896]{2,1,0:T(8,128)(2,1)}), bf16[4,48,896]{2,1,0:T(8,128)(2,1)}, u32[]{:S(2)}, u32[]{:S(2)}) %all-to-all-start.2) | async-done | bytes 344096 | tf_op jit(solution)/shard_map/all_to_all | solution.py:58
  86.7 3.5 %all-to-all-start.3 = ((bf16[4,48,896]{2,1,0:T(8,128)(2,1)}), bf16[4,48,896]{2,1,0:T(8,128)(2,1)S(1)}, u32[]{:S(2)}, u32[]{:S(2)}) async-start(bf16[4,48,896]{2,1,0:T(8,128)(2,1)} %broadcast_in_dim.37), calls=%async_computation.3 | async-start | bytes 688128 | tf_op jit(solution)/shard_map/all_to_all | solution.py:38
  90.2 3.8 %collective-permute-start.2 = (bf16[192,1792]{1,0:T(8,128)(2,1)S(1)}, bf16[192,1792]{1,0:T(8,128)(2,1)}, u32[]{:S(2)}, u32[]{:S(2)}) collective-permute-start(bf16[192,1792]{1,0:T(8,128)(2,1)S(1)} %copy-done.4), channel_id=1, source_target_pairs={{0,128},{128,256},{256,384},{384,0},{1,129},{129,257},{257,385},{3... | collective-permute-start | bytes 2064392 | tf_op jit(solution)/shard_map/ppermute | solution.py:44
  97.1 3.0 %all-to-all-done.3 = bf16[4,48,896]{2,1,0:T(8,128)(2,1)S(1)} async-done(((bf16[4,48,896]{2,1,0:T(8,128)(2,1)}), bf16[4,48,896]{2,1,0:T(8,128)(2,1)S(1)}, u32[]{:S(2)}, u32[]{:S(2)}) %all-to-all-start.3) | async-done | bytes 344096 | tf_op jit(solution)/shard_map/all_to_all | solution.py:38
  101.3 5.4 %all-to-all-start.4 = ((bf16[4,192,896]{2,1,0:T(8,128)(2,1)}), bf16[4,192,896]{2,1,0:T(8,128)(2,1)S(1)}, u32[]{:S(2)}, u32[]{:S(2)}) async-start(bf16[4,192,896]{2,1,0:T(8,128)(2,1)} %broadcast_in_dim.38), calls=%async_computation.4 | async-start | bytes 2752512 | tf_op jit(solution)/shard_map/all_to_all | solution.py:38
  106.7 2.6 %collective-permute-start.5 = (bf16[256,1792]{1,0:T(8,128)(2,1)}, bf16[256,1792]{1,0:T(8,128)(2,1)}, u32[]{:S(2)}, u32[]{:S(2)}) collective-permute-start(bf16[256,1792]{1,0:T(8,128)(2,1)} %pad_maximum_fusion.1), channel_id=1, source_target_pairs={{0,16},{16,0},{1,17},{17,1},{2,18},{18,2},{3,19},{19,3},{4,20},{20... | collective-permute-start | bytes 2752520 | tf_op jit(solution)/shard_map/ppermute | solution.py:20
  111.7 6.4 %collective-permute-done.4 = bf16[192,1792]{1,0:T(8,128)(2,1)} collective-permute-done((bf16[192,1792]{1,0:T(8,128)(2,1)}, bf16[192,1792]{1,0:T(8,128)(2,1)}, u32[]{:S(2)}, u32[]{:S(2)}) %collective-permute-start.4) | collective-permute-done | bytes 688160 | tf_op jit(solution)/shard_map/ppermute | solution.py:46
  120.5 2.8 %fusion.13 = (bf16[768,896]{1,0:T(8,128)(2,1)S(1)}, bf16[768,896]{1,0:T(8,128)(2,1)}, bf16[768,896]{1,0:T(8,128)(2,1)S(1)}) fusion(bf16[768,1792]{1,0:T(8,128)(2,1)S(1)} %bitcast.41), kind=kLoop, calls=%fused_computation.27 | loop fusion | flops 10321920 | bytes 6881280 | tf_op jit(solution)/shard_map/convert_element_type | solution.py:120
  126.7 2.2 %collective-permute-start.7 = (bf16[896,256]{1,0:T(8,128)(2,1)}, bf16[896,256]{1,0:T(8,128)(2,1)}, u32[]{:S(2)}, u32[]{:S(2)}) collective-permute-start(bf16[896,256]{1,0:T(8,128)(2,1)} %convolution_convert_fusion.2), channel_id=1, source_target_pairs={{0,16},{16,0},{1,17},{17,1},{2,18},{18,2},{3,19},{19,3},{4,20},{20... | collective-permute-start | bytes 1376264 | tf_op jit(solution)/shard_map/ppermute | solution.py:20
  132.9 3.9 %collective-permute-start.6 = (bf16[256,1792]{1,0:T(8,128)(2,1)}, bf16[256,1792]{1,0:T(8,128)(2,1)}, u32[]{:S(2)}, u32[]{:S(2)}) collective-permute-start(bf16[256,1792]{1,0:T(8,128)(2,1)} %convolution_convert_fusion), channel_id=1, source_target_pairs={{0,16},{16,0},{1,17},{17,1},{2,18},{18,2},{3,19},{19,3},{4,20},{20... | collective-permute-start | bytes 2752520 | tf_op jit(solution)/shard_map/ppermute | solution.py:20
  140.0 4.4 %all_to_all.35 = bf16[2,2,8,48,256]{4,3,2,1,0:T(8,128)(2,1)S(1)} all-to-all(bf16[2,2,8,48,256]{4,3,2,1,0:T(8,128)(2,1)S(1)} %maximum_select_fusion.1), channel_id=1, replica_groups=mesh['x'=4,'zq'=4,'zw'=2,'y'=8,'core'=2] {'core'}, dimensions={0} | all-to-all | bytes 1572864 | tf_op jit(solution)/shard_map/all_to_all | solution.py:136
  145.4 7.8 %all-to-all-start.6 = ((bf16[16,48,256]{2,1,0:T(8,128)(2,1)}), bf16[16,48,256]{2,1,0:T(8,128)(2,1)S(1)}, u32[]{:S(2)}, u32[]{:S(2)}) async-start(bf16[16,48,256]{2,1,0:T(8,128)(2,1)} %bitcast.22), calls=%async_computation.6 | async-start | bytes 786432 | tf_op jit(solution)/shard_map/all_to_all | solution.py:138
  155.3 2.4 %add_convert_fusion = bf16[896,256]{1,0:T(8,128)(2,1)} fusion(bf16[896,256]{1,0:T(8,128)(2,1)} %collective-permute-done.7, bf16[768,896]{1,0:T(8,128)(2,1)S(1)} %copy-done.9, bf16[768,512]{1,0:T(8,128)(2,1)S(1)} %bitcast.45), kind=kOutput, calls=%fused_computation.33 | convolution fusion | flops 353009664 | bytes 2686976 | tf_op jit(solution)/shard_map/dot_general | solution.py:12
  157.6 2.7 %add_convert_fusion.1 = (bf16[256,896]{1,0:T(8,128)(2,1)}, bf16[256,896]{1,0:T(8,128)(2,1)}) fusion(bf16[256,1792]{1,0:T(8,128)(2,1)} %collective-permute-done.6, f32[256,896]{1,0:T(8,128)S(1)} %fusion.11, bf16[768,256]{1,0:T(8,128)(2,1)S(1)} %copy-done.11, bf16[768,1792]{1,0:T(8,128)(2,1)S(1)} %copy-done.3), kind=kOutput, calls=%fused_computation.34 | convolution fusion | flops 353697792 | bytes 4521984 | tf_op jit(solution)/shard_map/dot_general | solution.py:12
  160.4 5.7 %all-to-all-done.6 = bf16[16,48,256]{2,1,0:T(8,128)(2,1)S(1)} async-done(((bf16[16,48,256]{2,1,0:T(8,128)(2,1)}), bf16[16,48,256]{2,1,0:T(8,128)(2,1)S(1)}, u32[]{:S(2)}, u32[]{:S(2)}) %all-to-all-start.6) | async-done | bytes 393248 | tf_op jit(solution)/shard_map/all_to_all | solution.py:138
  (73 shorter events, 32.6 us)
Async XLA Ops:
  2.4 30.5 %all-to-all-start = ((bf16[16,48,512]{2,1,0:T(8,128)(2,1)}), bf16[16,48,512]{2,1,0:T(8,128)(2,1)S(1)}, u32[]{:S(2)}, u32[]{:S(2)}) async-start(bf16[16,48,512]{2,1,0:T(8,128)(2,1)} %bitcast.1), calls=%async_computation | async-start | bytes 1572864 | tf_op jit(solution)/shard_map/all_to_all | solution.py:82
  11.8 21.2 %collective-permute-start = (bf16[896,256]{1,0:T(8,128)(2,1)}, bf16[896,256]{1,0:T(8,128)(2,1)S(1)}, u32[]{:S(2)}, u32[]{:S(2)}) collective-permute-start(bf16[896,256]{1,0:T(8,128)(2,1)} %param.13), channel_id=1, source_target_pairs={{0,16},{16,0},{1,17},{17,1},{2,18},{18,2},{3,19},{19,3},{4,20},{20... | collective-permute-start | bytes 1376264 | tf_op jit(solution)/shard_map/ppermute | solution.py:20
  33.0 4.2 %collective-permute-start.1 = (bf16[2,8,1,48,512]{4,3,2,1,0:T(8,128)(2,1)S(1)}, bf16[2,8,1,48,512]{4,3,2,1,0:T(8,128)(2,1)S(1)}, u32[]{:S(2)}, u32[]{:S(2)}) collective-permute-start(bf16[2,8,1,48,512]{4,3,2,1,0:T(8,128)(2,1)S(1)} %bitcast.49), channel_id=1, source_target_pairs={{0,1},{1,0},{2,3},{3,2},{4,5},{5,4},{6,7},{7,6},{8,9},{9,8},{10,11... | collective-permute-start | bytes 2359304 | tf_op jit(solution)/shard_map/ppermute | solution.py:87
  37.5 40.9 %copy-start = (bf16[1,8,2,48,512]{4,3,2,1,0:T(8,128)(2,1)}, bf16[1,8,2,48,512]{4,3,2,1,0:T(8,128)(2,1)S(1)}, u32[]{:S(2)}) copy-start(bf16[1,8,2,48,512]{4,3,2,1,0:T(8,128)(2,1)S(1)} %get-tuple-element.70) | copy-start | bytes 2359300
  38.3 6.9 %copy-start.13 = (bf16[48,896]{1,0:T(8,128)(2,1)S(1)}, bf16[48,896]{1,0:T(8,128)(2,1)}, u32[]{:S(2)}) copy-start(bf16[48,896]{1,0:T(8,128)(2,1)} %param.10) | copy-start | bytes 258052
  38.3 6.9 %copy-start.14 = (bf16[48,896]{1,0:T(8,128)(2,1)S(1)}, bf16[48,896]{1,0:T(8,128)(2,1)}, u32[]{:S(2)}) copy-start(bf16[48,896]{1,0:T(8,128)(2,1)} %param.9) | copy-start | bytes 258052
  40.4 27.8 %all-to-all-start.1 = ((bf16[4,192,896]{2,1,0:T(8,128)(2,1)}), bf16[4,192,896]{2,1,0:T(8,128)(2,1)S(1)}, u32[]{:S(2)}, u32[]{:S(2)}) async-start(bf16[4,192,896]{2,1,0:T(8,128)(2,1)} %bitcast.51), calls=%async_computation.1 | async-start | bytes 2752512 | tf_op jit(solution)/shard_map/all_to_all | solution.py:58
  68.2 25.8 %copy-start.5 = (bf16[256,896]{1,0:T(8,128)(2,1)S(1)}, bf16[256,896]{1,0:T(8,128)(2,1)}, u32[]{:S(2)}) copy-start(bf16[256,896]{1,0:T(8,128)(2,1)} %param.12) | copy-start | bytes 1376260
  69.2 21.0 %copy-start.4 = (bf16[192,1792]{1,0:T(8,128)(2,1)S(1)}, bf16[192,1792]{1,0:T(8,128)(2,1)}, u32[]{:S(2)}) copy-start(bf16[192,1792]{1,0:T(8,128)(2,1)} %all_gather.3) | copy-start | bytes 2064388
  69.2 24.8 %copy-start.6 = (bf16[256,896]{1,0:T(8,128)(2,1)S(1)}, bf16[256,896]{1,0:T(8,128)(2,1)}, u32[]{:S(2)}) copy-start(bf16[256,896]{1,0:T(8,128)(2,1)} %param.11) | copy-start | bytes 1376260
  69.2 15.6 %all-to-all-start.2 = ((bf16[4,48,896]{2,1,0:T(8,128)(2,1)}), bf16[4,48,896]{2,1,0:T(8,128)(2,1)}, u32[]{:S(2)}, u32[]{:S(2)}) async-start(bf16[4,48,896]{2,1,0:T(8,128)(2,1)} %bitcast.53), calls=%async_computation.2 | async-start | bytes 688128 | tf_op jit(solution)/shard_map/all_to_all | solution.py:58
  75.0 20.0 %collective-permute-start.3 = (bf16[192,1792]{1,0:T(8,128)(2,1)}, bf16[192,1792]{1,0:T(8,128)(2,1)}, u32[]{:S(2)}, u32[]{:S(2)}) collective-permute-start(bf16[192,1792]{1,0:T(8,128)(2,1)} %all_gather.3), channel_id=1, source_target_pairs={{0,384},{128,0},{256,128},{384,256},{1,385},{129,1},{257,129},{385... | collective-permute-start | bytes 2064392 | tf_op jit(solution)/shard_map/ppermute | solution.py:45
  86.7 13.4 %all-to-all-start.3 = ((bf16[4,48,896]{2,1,0:T(8,128)(2,1)}), bf16[4,48,896]{2,1,0:T(8,128)(2,1)S(1)}, u32[]{:S(2)}, u32[]{:S(2)}) async-start(bf16[4,48,896]{2,1,0:T(8,128)(2,1)} %broadcast_in_dim.37), calls=%async_computation.3 | async-start | bytes 688128 | tf_op jit(solution)/shard_map/all_to_all | solution.py:38
  90.2 20.4 %collective-permute-start.2 = (bf16[192,1792]{1,0:T(8,128)(2,1)S(1)}, bf16[192,1792]{1,0:T(8,128)(2,1)}, u32[]{:S(2)}, u32[]{:S(2)}) collective-permute-start(bf16[192,1792]{1,0:T(8,128)(2,1)S(1)} %copy-done.4), channel_id=1, source_target_pairs={{0,128},{128,256},{256,384},{384,0},{1,129},{129,257},{257,385},{3... | collective-permute-start | bytes 2064392 | tf_op jit(solution)/shard_map/ppermute | solution.py:44
  95.0 23.1 %collective-permute-start.4 = (bf16[192,1792]{1,0:T(8,128)(2,1)}, bf16[192,1792]{1,0:T(8,128)(2,1)}, u32[]{:S(2)}, u32[]{:S(2)}) collective-permute-start(bf16[192,1792]{1,0:T(8,128)(2,1)} %collective-permute-done.3), channel_id=1, source_target_pairs={{0,384},{128,0},{256,128},{384,256},{1,385},{129,1},{257,129},{385... | collective-permute-start | bytes 2064392 | tf_op jit(solution)/shard_map/ppermute | solution.py:46
  101.3 25.3 %all-to-all-start.4 = ((bf16[4,192,896]{2,1,0:T(8,128)(2,1)}), bf16[4,192,896]{2,1,0:T(8,128)(2,1)S(1)}, u32[]{:S(2)}, u32[]{:S(2)}) async-start(bf16[4,192,896]{2,1,0:T(8,128)(2,1)} %broadcast_in_dim.38), calls=%async_computation.4 | async-start | bytes 2752512 | tf_op jit(solution)/shard_map/all_to_all | solution.py:38
  106.7 31.1 %collective-permute-start.5 = (bf16[256,1792]{1,0:T(8,128)(2,1)}, bf16[256,1792]{1,0:T(8,128)(2,1)}, u32[]{:S(2)}, u32[]{:S(2)}) collective-permute-start(bf16[256,1792]{1,0:T(8,128)(2,1)} %pad_maximum_fusion.1), channel_id=1, source_target_pairs={{0,16},{16,0},{1,17},{17,1},{2,18},{18,2},{3,19},{19,3},{4,20},{20... | collective-permute-start | bytes 2752520 | tf_op jit(solution)/shard_map/ppermute | solution.py:20
  126.7 28.6 %collective-permute-start.7 = (bf16[896,256]{1,0:T(8,128)(2,1)}, bf16[896,256]{1,0:T(8,128)(2,1)}, u32[]{:S(2)}, u32[]{:S(2)}) collective-permute-start(bf16[896,256]{1,0:T(8,128)(2,1)} %convolution_convert_fusion.2), channel_id=1, source_target_pairs={{0,16},{16,0},{1,17},{17,1},{2,18},{18,2},{3,19},{19,3},{4,20},{20... | collective-permute-start | bytes 1376264 | tf_op jit(solution)/shard_map/ppermute | solution.py:20
  132.9 4.9 %copy-start.2 = (bf16[768,1792]{1,0:T(8,128)(2,1)}, bf16[768,1792]{1,0:T(8,128)(2,1)S(1)}, u32[]{:S(2)}) copy-start(bf16[768,1792]{1,0:T(8,128)(2,1)S(1)} %pad_maximum_fusion) | copy-start | bytes 8257540
  132.9 24.7 %collective-permute-start.6 = (bf16[256,1792]{1,0:T(8,128)(2,1)}, bf16[256,1792]{1,0:T(8,128)(2,1)}, u32[]{:S(2)}, u32[]{:S(2)}) collective-permute-start(bf16[256,1792]{1,0:T(8,128)(2,1)} %convolution_convert_fusion), channel_id=1, source_target_pairs={{0,16},{16,0},{1,17},{17,1},{2,18},{18,2},{3,19},{19,3},{4,20},{20... | collective-permute-start | bytes 2752520 | tf_op jit(solution)/shard_map/ppermute | solution.py:20
  139.9 13.2 %copy-start.11 = (bf16[768,256]{1,0:T(8,128)(2,1)S(1)}, bf16[768,256]{1,0:T(8,128)(2,1)}, u32[]{:S(2)}) copy-start(bf16[768,256]{1,0:T(8,128)(2,1)} %slice.32) | copy-start | bytes 1179652
  144.4 10.9 %copy-start.9 = (bf16[768,896]{1,0:T(8,128)(2,1)S(1)}, bf16[768,896]{1,0:T(8,128)(2,1)}, u32[]{:S(2)}) copy-start(bf16[768,896]{1,0:T(8,128)(2,1)} %copy-done.8) | copy-start | bytes 4128772
  145.4 20.6 %all-to-all-start.6 = ((bf16[16,48,256]{2,1,0:T(8,128)(2,1)}), bf16[16,48,256]{2,1,0:T(8,128)(2,1)S(1)}, u32[]{:S(2)}, u32[]{:S(2)}) async-start(bf16[16,48,256]{2,1,0:T(8,128)(2,1)} %bitcast.22), calls=%async_computation.6 | async-start | bytes 786432 | tf_op jit(solution)/shard_map/all_to_all | solution.py:138
  153.2 4.5 %copy-start.3 = (bf16[768,1792]{1,0:T(8,128)(2,1)S(1)}, bf16[768,1792]{1,0:T(8,128)(2,1)}, u32[]{:S(2)}) copy-start(bf16[768,1792]{1,0:T(8,128)(2,1)} %copy-done.2) | copy-start | bytes 8257540
  (6 other events, 17.1 us)

commit v6 on v4

--- a/solution.py
+++ b/solution.py
@@ -101,7 +101,7 @@
     own, other = own[:, width:], other[:, width:]
     part = scatter_sum(part.reshape(4, tokens, units), "zq").astype(BF)
     both_w = jnp.concatenate([gate_weight, up_weight], axis=1)
-    part, own, other = tie(part, own, other)
+    part, own, other, both_w = tie(part, own, other, both_w)
     hidden_grad = spread(part, "zq", 4)
     hidden_grad, both_w, pre, gate_weight, up_weight = tie(
         hidden_grad, both_w, pre, gate_weight, up_weight

time: 168 us -> 170 us (1.012)
  other arithmetic: 9.69 us -> 11.6 us
    all_to_all x2, waiting for transfers between devices: 5.52 us -> 3.32 us  [scatter_sum(): return lax.all_to_all(value, axis, 0, 0, tiled=True).astype(F32).sum(axis=0)]
  transfers between devices with their start and end apart: 14 -> 14, of which waited for: 7 -> 8; matrix products, arithmetic and copies ran while one was open for 17% -> 18% of each run, Pallas kernels for 0% -> 0%
where the time goes in v6:
time: 170 us; the launch traced here: 168 us
  starting transfers between devices  60.6 us (36%)
  waiting for transfers between devices  40.7 us (24%)
  blocking collectives  27.3 us (16%)
  matrix products  15.6 us (9%)
  other arithmetic  11.6 us (7%)
  local copies, waits for them, and re-layouts  11.5 us (7%)
    all_gather x1, blocking collectives, body(): pre = lax.all_gather(pre, 'zq', axis=0, tiled=True)  23 us
    ppermute x4, waiting for transfers between devices, swap(): return lax.ppermute(value, 'zw', SWAP)  17.8 us
    ppermute x4, starting transfers between devices, swap(): return lax.ppermute(value, 'zw', SWAP)  11.8 us
    all_to_all x2, starting transfers between devices, spread(): lax.all_to_all(copies, axis, 0, 0, tiled=True)  10.8 us
    dot_general x5, matrix products, contract_rows(): lax.dot_general(left, right, (((0,), (0,)), ((), ())), preferred_element_...  10.5 us
    all_to_all x2, starting transfers between devices, scatter_sum(): return lax.all_to_all(value, axis, 0, 0, tiled=True).astype(F32).sum(axis=0)  10.2 us
    all_to_all x1, starting transfers between devices, body(): rows = lax.all_to_all(rows, ('zw', 'y'), 0, 0, tiled=True)  9.37 us
    all_to_all x1, starting transfers between devices, body(): term = lax.all_to_all(term, ('zw', 'y'), 0, 0, tiled=True)  7.49 us
  transfers between devices with their start and end apart: 14, of which 8 were waited for; matrix products, arithmetic and copies ran while one was open for 18% of the time, Pallas kernels for 0%

profile of v6, /device:TPU:14, one launch (start us, length us, event | category | flops | bytes accessed | tf_op | source)
XLA Modules:
  0.0 168.3 jit_solution(16361282590163121887)
XLA Ops:
  2.4 9.4 %all-to-all-start = ((bf16[16,48,512]{2,1,0:T(8,128)(2,1)}), bf16[16,48,512]{2,1,0:T(8,128)(2,1)S(1)}, u32[]{:S(2)}, u32[]{:S(2)}) async-start(bf16[16,48,512]{2,1,0:T(8,128)(2,1)} %bitcast.1), calls=%async_computation | async-start | bytes 1572864 | tf_op jit(solution)/shard_map/all_to_all | solution.py:82
  11.8 3.4 %collective-permute-start = (bf16[896,256]{1,0:T(8,128)(2,1)}, bf16[896,256]{1,0:T(8,128)(2,1)S(1)}, u32[]{:S(2)}, u32[]{:S(2)}) collective-permute-start(bf16[896,256]{1,0:T(8,128)(2,1)} %param.13), channel_id=1, source_target_pairs={{0,16},{16,0},{1,17},{17,1},{2,18},{18,2},{3,19},{19,3},{4,20},{20... | collective-permute-start | bytes 1376264 | tf_op jit(solution)/shard_map/ppermute | solution.py:20
  15.2 17.8 %collective-permute-done = bf16[896,256]{1,0:T(8,128)(2,1)S(1)} collective-permute-done((bf16[896,256]{1,0:T(8,128)(2,1)}, bf16[896,256]{1,0:T(8,128)(2,1)S(1)}, u32[]{:S(2)}, u32[]{:S(2)}) %collective-permute-start) | collective-permute-done | bytes 458784 | tf_op jit(solution)/shard_map/ppermute | solution.py:20
  34.9 2.2 %collective-permute-done.1 = bf16[2,8,1,48,512]{4,3,2,1,0:T(8,128)(2,1)S(1)} collective-permute-done((bf16[2,8,1,48,512]{4,3,2,1,0:T(8,128)(2,1)S(1)}, bf16[2,8,1,48,512]{4,3,2,1,0:T(8,128)(2,1)S(1)}, u32[]{:S(2)}, u32[]{:S(2)}) %collective-permute-start.1) | collective-permute-done | bytes 786464 | tf_op jit(solution)/shard_map/ppermute | solution.py:87
  40.4 4.8 %all-to-all-start.1 = ((bf16[4,192,896]{2,1,0:T(8,128)(2,1)}), bf16[4,192,896]{2,1,0:T(8,128)(2,1)S(1)}, u32[]{:S(2)}, u32[]{:S(2)}) async-start(bf16[4,192,896]{2,1,0:T(8,128)(2,1)} %bitcast.51), calls=%async_computation.1 | async-start | bytes 2752512 | tf_op jit(solution)/shard_map/all_to_all | solution.py:58
  46.2 23.0 %all_gather.3 = bf16[192,1792]{1,0:T(8,128)(2,1)} all-gather(bf16[48,1792]{1,0:T(8,128)(2,1)S(1)} %pad_maximum_fusion.3), channel_id=1, replica_groups=mesh['x'=4,'zq'=4,'zw'=2,'y'=8,'core'=2] {'zq'}, dimensions={0}, use_global_device_ids=true | all-gather | bytes 860160 | tf_op jit(solution)/shard_map/all_gather | solution.py:97
  70.2 5.5 %all-to-all-start.2 = ((bf16[4,48,896]{2,1,0:T(8,128)(2,1)}), bf16[4,48,896]{2,1,0:T(8,128)(2,1)S(1)}, u32[]{:S(2)}, u32[]{:S(2)}) async-start(bf16[4,48,896]{2,1,0:T(8,128)(2,1)} %bitcast.53), calls=%async_computation.2 | async-start | bytes 688128 | tf_op jit(solution)/shard_map/all_to_all | solution.py:58
  77.2 2.7 %collective-permute-start.3 = (bf16[192,1792]{1,0:T(8,128)(2,1)}, bf16[192,1792]{1,0:T(8,128)(2,1)}, u32[]{:S(2)}, u32[]{:S(2)}) collective-permute-start(bf16[192,1792]{1,0:T(8,128)(2,1)} %all_gather.3), channel_id=1, source_target_pairs={{0,384},{128,0},{256,128},{384,256},{1,385},{129,1},{257,129},{385... | collective-permute-start | bytes 2064392 | tf_op jit(solution)/shard_map/ppermute | solution.py:45
  82.0 3.3 %all-to-all-done.2 = bf16[4,48,896]{2,1,0:T(8,128)(2,1)S(1)} async-done(((bf16[4,48,896]{2,1,0:T(8,128)(2,1)}), bf16[4,48,896]{2,1,0:T(8,128)(2,1)S(1)}, u32[]{:S(2)}, u32[]{:S(2)}) %all-to-all-start.2) | async-done | bytes 344096 | tf_op jit(solution)/shard_map/all_to_all | solution.py:58
  86.1 3.9 %all-to-all-start.3 = ((bf16[4,48,896]{2,1,0:T(8,128)(2,1)}), bf16[4,48,896]{2,1,0:T(8,128)(2,1)S(1)}, u32[]{:S(2)}, u32[]{:S(2)}) async-start(bf16[4,48,896]{2,1,0:T(8,128)(2,1)} %broadcast_in_dim.37), calls=%async_computation.3 | async-start | bytes 688128 | tf_op jit(solution)/shard_map/all_to_all | solution.py:38
  90.0 4.3 %collective-permute-start.2 = (bf16[192,1792]{1,0:T(8,128)(2,1)}, bf16[192,1792]{1,0:T(8,128)(2,1)}, u32[]{:S(2)}, u32[]{:S(2)}) collective-permute-start(bf16[192,1792]{1,0:T(8,128)(2,1)} %all_gather.3), channel_id=1, source_target_pairs={{0,128},{128,256},{256,384},{384,0},{1,129},{129,257},{257,385},{3... | collective-permute-start | bytes 2064392 | tf_op jit(solution)/shard_map/ppermute | solution.py:44
  97.5 2.7 %all-to-all-done.3 = bf16[4,48,896]{2,1,0:T(8,128)(2,1)S(1)} async-done(((bf16[4,48,896]{2,1,0:T(8,128)(2,1)}), bf16[4,48,896]{2,1,0:T(8,128)(2,1)S(1)}, u32[]{:S(2)}, u32[]{:S(2)}) %all-to-all-start.3) | async-done | bytes 344096 | tf_op jit(solution)/shard_map/all_to_all | solution.py:38
  101.3 7.0 %all-to-all-start.4 = ((bf16[4,192,896]{2,1,0:T(8,128)(2,1)}), bf16[4,192,896]{2,1,0:T(8,128)(2,1)}, u32[]{:S(2)}, u32[]{:S(2)}) async-start(bf16[4,192,896]{2,1,0:T(8,128)(2,1)} %broadcast_in_dim.38), calls=%async_computation.4 | async-start | bytes 2752512 | tf_op jit(solution)/shard_map/all_to_all | solution.py:38
  108.3 2.4 %collective-permute-start.5 = (bf16[256,1792]{1,0:T(8,128)(2,1)}, bf16[256,1792]{1,0:T(8,128)(2,1)}, u32[]{:S(2)}, u32[]{:S(2)}) collective-permute-start(bf16[256,1792]{1,0:T(8,128)(2,1)} %pad_maximum_fusion.1), channel_id=1, source_target_pairs={{0,16},{16,0},{1,17},{17,1},{2,18},{18,2},{3,19},{19,3},{4,20},{20... | collective-permute-start | bytes 2752520 | tf_op jit(solution)/shard_map/ppermute | solution.py:20
  114.2 5.5 %collective-permute-done.4 = bf16[192,1792]{1,0:T(8,128)(2,1)} collective-permute-done((bf16[192,1792]{1,0:T(8,128)(2,1)}, bf16[192,1792]{1,0:T(8,128)(2,1)}, u32[]{:S(2)}, u32[]{:S(2)}) %collective-permute-start.4) | collective-permute-done | bytes 688160 | tf_op jit(solution)/shard_map/ppermute | solution.py:46
  125.4 2.3 %all-to-all-done.4 = bf16[4,192,896]{2,1,0:T(8,128)(2,1)} async-done(((bf16[4,192,896]{2,1,0:T(8,128)(2,1)}), bf16[4,192,896]{2,1,0:T(8,128)(2,1)}, u32[]{:S(2)}, u32[]{:S(2)}) %all-to-all-start.4) | async-done | bytes 1376288 | tf_op jit(solution)/shard_map/all_to_all | solution.py:38
  129.8 2.8 %fusion.6 = (bf16[768,896]{1,0:T(8,128)(2,1)S(1)}, bf16[768,896]{1,0:T(8,128)(2,1)S(1)}) fusion(bf16[768,896]{1,0:T(8,128)(2,1)} %bitcast.8, bf16[768,1792]{1,0:T(8,128)(2,1)S(1)} %bitcast.42), kind=kLoop, calls=%fused_computation.13 | loop fusion | flops 11010048 | bytes 6881280 | tf_op jit(solution)/shard_map/convert_element_type | solution.py:130
  134.7 4.1 %collective-permute-start.6 = (bf16[256,1792]{1,0:T(8,128)(2,1)}, bf16[256,1792]{1,0:T(8,128)(2,1)}, u32[]{:S(2)}, u32[]{:S(2)}) collective-permute-start(bf16[256,1792]{1,0:T(8,128)(2,1)} %convolution_convert_fusion), channel_id=1, source_target_pairs={{0,16},{16,0},{1,17},{17,1},{2,18},{18,2},{3,19},{19,3},{4,20},{20... | collective-permute-start | bytes 2752520 | tf_op jit(solution)/shard_map/ppermute | solution.py:20
  141.9 4.4 %all_to_all.35 = bf16[2,2,8,48,256]{4,3,2,1,0:T(8,128)(2,1)S(1)} all-to-all(bf16[2,2,8,48,256]{4,3,2,1,0:T(8,128)(2,1)S(1)} %maximum_select_fusion.1), channel_id=1, replica_groups=mesh['x'=4,'zq'=4,'zw'=2,'y'=8,'core'=2] {'core'}, dimensions={0} | all-to-all | bytes 1572864 | tf_op jit(solution)/shard_map/all_to_all | solution.py:137
  147.3 7.5 %all-to-all-start.6 = ((bf16[16,48,256]{2,1,0:T(8,128)(2,1)}), bf16[16,48,256]{2,1,0:T(8,128)(2,1)S(1)}, u32[]{:S(2)}, u32[]{:S(2)}) async-start(bf16[16,48,256]{2,1,0:T(8,128)(2,1)} %bitcast.22), calls=%async_computation.6 | async-start | bytes 786432 | tf_op jit(solution)/shard_map/all_to_all | solution.py:139
  154.8 2.2 %fusion.15 = f32[256,896]{1,0:T(8,128)S(1)} fusion(bf16[768,256]{1,0:T(8,128)(2,1)} %slice.38, bf16[768,1792]{1,0:T(8,128)(2,1)} %copy-done.2), kind=kOutput, calls=%fused_computation.26 | convolution fusion | flops 352321536 | bytes 2686976 | tf_op jit(solution)/shard_map/dot_general | solution.py:12
  157.0 2.4 %add_convert_fusion = bf16[896,256]{1,0:T(8,128)(2,1)} fusion(bf16[896,256]{1,0:T(8,128)(2,1)} %collective-permute-done.7, bf16[768,896]{1,0:T(8,128)(2,1)S(1)} %copy-done.8, bf16[768,512]{1,0:T(8,128)(2,1)S(1)} %bitcast.45), kind=kOutput, calls=%fused_computation.36 | convolution fusion | flops 353009664 | bytes 2686976 | tf_op jit(solution)/shard_map/dot_general | solution.py:12
  159.4 2.7 %add_convert_fusion.1 = (bf16[256,896]{1,0:T(8,128)(2,1)}, bf16[256,896]{1,0:T(8,128)(2,1)}) fusion(bf16[256,1792]{1,0:T(8,128)(2,1)} %collective-permute-done.6, f32[256,896]{1,0:T(8,128)S(1)} %fusion.15, bf16[768,256]{1,0:T(8,128)(2,1)S(1)} %copy-done.10, bf16[768,1792]{1,0:T(8,128)(2,1)S(1)} %copy-done.3), kind=kOutput, calls=%fused_computation.37 | convolution fusion | flops 353697792 | bytes 4521984 | tf_op jit(solution)/shard_map/dot_general | solution.py:12
  162.1 5.5 %all-to-all-done.6 = bf16[16,48,256]{2,1,0:T(8,128)(2,1)S(1)} async-done(((bf16[16,48,256]{2,1,0:T(8,128)(2,1)}), bf16[16,48,256]{2,1,0:T(8,128)(2,1)S(1)}, u32[]{:S(2)}, u32[]{:S(2)}) %all-to-all-start.6) | async-done | bytes 393248 | tf_op jit(solution)/shard_map/all_to_all | solution.py:139
  (69 shorter events, 35.8 us)
Async XLA Ops:
  2.4 30.5 %all-to-all-start = ((bf16[16,48,512]{2,1,0:T(8,128)(2,1)}), bf16[16,48,512]{2,1,0:T(8,128)(2,1)S(1)}, u32[]{:S(2)}, u32[]{:S(2)}) async-start(bf16[16,48,512]{2,1,0:T(8,128)(2,1)} %bitcast.1), calls=%async_computation | async-start | bytes 1572864 | tf_op jit(solution)/shard_map/all_to_all | solution.py:82
  11.8 21.2 %collective-permute-start = (bf16[896,256]{1,0:T(8,128)(2,1)}, bf16[896,256]{1,0:T(8,128)(2,1)S(1)}, u32[]{:S(2)}, u32[]{:S(2)}) collective-permute-start(bf16[896,256]{1,0:T(8,128)(2,1)} %param.13), channel_id=1, source_target_pairs={{0,16},{16,0},{1,17},{17,1},{2,18},{18,2},{3,19},{19,3},{4,20},{20... | collective-permute-start | bytes 1376264 | tf_op jit(solution)/shard_map/ppermute | solution.py:20
  33.0 4.2 %collective-permute-start.1 = (bf16[2,8,1,48,512]{4,3,2,1,0:T(8,128)(2,1)S(1)}, bf16[2,8,1,48,512]{4,3,2,1,0:T(8,128)(2,1)S(1)}, u32[]{:S(2)}, u32[]{:S(2)}) collective-permute-start(bf16[2,8,1,48,512]{4,3,2,1,0:T(8,128)(2,1)S(1)} %bitcast.49), channel_id=1, source_target_pairs={{0,1},{1,0},{2,3},{3,2},{4,5},{5,4},{6,7},{7,6},{8,9},{9,8},{10,11... | collective-permute-start | bytes 2359304 | tf_op jit(solution)/shard_map/ppermute | solution.py:87
  37.5 39.0 %copy-start = (bf16[1,8,2,48,512]{4,3,2,1,0:T(8,128)(2,1)}, bf16[1,8,2,48,512]{4,3,2,1,0:T(8,128)(2,1)S(1)}, u32[]{:S(2)}) copy-start(bf16[1,8,2,48,512]{4,3,2,1,0:T(8,128)(2,1)S(1)} %get-tuple-element.69) | copy-start | bytes 2359300
  38.3 6.9 %copy-start.12 = (bf16[48,896]{1,0:T(8,128)(2,1)S(1)}, bf16[48,896]{1,0:T(8,128)(2,1)}, u32[]{:S(2)}) copy-start(bf16[48,896]{1,0:T(8,128)(2,1)} %param.10) | copy-start | bytes 258052
  40.4 28.7 %all-to-all-start.1 = ((bf16[4,192,896]{2,1,0:T(8,128)(2,1)}), bf16[4,192,896]{2,1,0:T(8,128)(2,1)S(1)}, u32[]{:S(2)}, u32[]{:S(2)}) async-start(bf16[4,192,896]{2,1,0:T(8,128)(2,1)} %bitcast.51), calls=%async_computation.1 | async-start | bytes 2752512 | tf_op jit(solution)/shard_map/all_to_all | solution.py:58
  45.2 34.7 %copy-start.4 = (bf16[256,896]{1,0:T(8,128)(2,1)S(1)}, bf16[256,896]{1,0:T(8,128)(2,1)}, u32[]{:S(2)}) copy-start(bf16[256,896]{1,0:T(8,128)(2,1)} %param.12) | copy-start | bytes 1376260
  70.2 15.1 %all-to-all-start.2 = ((bf16[4,48,896]{2,1,0:T(8,128)(2,1)}), bf16[4,48,896]{2,1,0:T(8,128)(2,1)S(1)}, u32[]{:S(2)}, u32[]{:S(2)}) async-start(bf16[4,48,896]{2,1,0:T(8,128)(2,1)} %bitcast.53), calls=%async_computation.2 | async-start | bytes 688128 | tf_op jit(solution)/shard_map/all_to_all | solution.py:58
  77.2 18.4 %collective-permute-start.3 = (bf16[192,1792]{1,0:T(8,128)(2,1)}, bf16[192,1792]{1,0:T(8,128)(2,1)}, u32[]{:S(2)}, u32[]{:S(2)}) collective-permute-start(bf16[192,1792]{1,0:T(8,128)(2,1)} %all_gather.3), channel_id=1, source_target_pairs={{0,384},{128,0},{256,128},{384,256},{1,385},{129,1},{257,129},{385... | collective-permute-start | bytes 2064392 | tf_op jit(solution)/shard_map/ppermute | solution.py:45
  86.1 14.0 %all-to-all-start.3 = ((bf16[4,48,896]{2,1,0:T(8,128)(2,1)}), bf16[4,48,896]{2,1,0:T(8,128)(2,1)S(1)}, u32[]{:S(2)}, u32[]{:S(2)}) async-start(bf16[4,48,896]{2,1,0:T(8,128)(2,1)} %broadcast_in_dim.37), calls=%async_computation.3 | async-start | bytes 688128 | tf_op jit(solution)/shard_map/all_to_all | solution.py:38
  90.0 23.1 %collective-permute-start.2 = (bf16[192,1792]{1,0:T(8,128)(2,1)}, bf16[192,1792]{1,0:T(8,128)(2,1)}, u32[]{:S(2)}, u32[]{:S(2)}) collective-permute-start(bf16[192,1792]{1,0:T(8,128)(2,1)} %all_gather.3), channel_id=1, source_target_pairs={{0,128},{128,256},{256,384},{384,0},{1,129},{129,257},{257,385},{3... | collective-permute-start | bytes 2064392 | tf_op jit(solution)/shard_map/ppermute | solution.py:44
  95.5 24.2 %collective-permute-start.4 = (bf16[192,1792]{1,0:T(8,128)(2,1)}, bf16[192,1792]{1,0:T(8,128)(2,1)}, u32[]{:S(2)}, u32[]{:S(2)}) collective-permute-start(bf16[192,1792]{1,0:T(8,128)(2,1)} %collective-permute-done.3), channel_id=1, source_target_pairs={{0,384},{128,0},{256,128},{384,256},{1,385},{129,1},{257,129},{385... | collective-permute-start | bytes 2064392 | tf_op jit(solution)/shard_map/ppermute | solution.py:46
  101.3 26.4 %all-to-all-start.4 = ((bf16[4,192,896]{2,1,0:T(8,128)(2,1)}), bf16[4,192,896]{2,1,0:T(8,128)(2,1)}, u32[]{:S(2)}, u32[]{:S(2)}) async-start(bf16[4,192,896]{2,1,0:T(8,128)(2,1)} %broadcast_in_dim.38), calls=%async_computation.4 | async-start | bytes 2752512 | tf_op jit(solution)/shard_map/all_to_all | solution.py:38
  108.3 3.7 %copy-start.6 = (bf16[256,896]{1,0:T(8,128)(2,1)S(1)}, bf16[256,896]{1,0:T(8,128)(2,1)}, u32[]{:S(2)}) copy-start(bf16[256,896]{1,0:T(8,128)(2,1)} %param.11) | copy-start | bytes 1376260
  108.3 31.3 %collective-permute-start.5 = (bf16[256,1792]{1,0:T(8,128)(2,1)}, bf16[256,1792]{1,0:T(8,128)(2,1)}, u32[]{:S(2)}, u32[]{:S(2)}) collective-permute-start(bf16[256,1792]{1,0:T(8,128)(2,1)} %pad_maximum_fusion.1), channel_id=1, source_target_pairs={{0,16},{16,0},{1,17},{17,1},{2,18},{18,2},{3,19},{19,3},{4,20},{20... | collective-permute-start | bytes 2752520 | tf_op jit(solution)/shard_map/ppermute | solution.py:20
  127.7 4.9 %copy-start.11 = (bf16[768,256]{1,0:T(8,128)(2,1)S(1)}, bf16[768,256]{1,0:T(8,128)(2,1)}, u32[]{:S(2)}) copy-start(bf16[768,256]{1,0:T(8,128)(2,1)} %slice.39) | copy-start | bytes 1179652
  127.7 29.3 %collective-permute-start.7 = (bf16[896,256]{1,0:T(8,128)(2,1)}, bf16[896,256]{1,0:T(8,128)(2,1)}, u32[]{:S(2)}, u32[]{:S(2)}) collective-permute-start(bf16[896,256]{1,0:T(8,128)(2,1)} %convolution_convert_fusion.2), channel_id=1, source_target_pairs={{0,16},{16,0},{1,17},{17,1},{2,18},{18,2},{3,19},{19,3},{4,20},{20... | collective-permute-start | bytes 1376264 | tf_op jit(solution)/shard_map/ppermute | solution.py:20
  134.5 4.3 %copy-start.9 = (bf16[256,1792]{1,0:T(8,128)(2,1)S(1)}, bf16[256,1792]{1,0:T(8,128)(2,1)}, u32[]{:S(2)}) copy-start(bf16[256,1792]{1,0:T(8,128)(2,1)} %pad_maximum_fusion.2) | copy-start | bytes 2752516
  134.7 5.0 %copy-start.2 = (bf16[768,1792]{1,0:T(8,128)(2,1)}, bf16[768,1792]{1,0:T(8,128)(2,1)S(1)}, u32[]{:S(2)}) copy-start(bf16[768,1792]{1,0:T(8,128)(2,1)S(1)} %pad_maximum_fusion) | copy-start | bytes 8257540
  134.7 24.7 %collective-permute-start.6 = (bf16[256,1792]{1,0:T(8,128)(2,1)}, bf16[256,1792]{1,0:T(8,128)(2,1)}, u32[]{:S(2)}, u32[]{:S(2)}) collective-permute-start(bf16[256,1792]{1,0:T(8,128)(2,1)} %convolution_convert_fusion), channel_id=1, source_target_pairs={{0,16},{16,0},{1,17},{17,1},{2,18},{18,2},{3,19},{19,3},{4,20},{20... | collective-permute-start | bytes 2752520 | tf_op jit(solution)/shard_map/ppermute | solution.py:20
  146.3 10.7 %copy-start.8 = (bf16[768,896]{1,0:T(8,128)(2,1)S(1)}, bf16[768,896]{1,0:T(8,128)(2,1)}, u32[]{:S(2)}) copy-start(bf16[768,896]{1,0:T(8,128)(2,1)} %copy-done.7) | copy-start | bytes 4128772
  147.3 20.4 %all-to-all-start.6 = ((bf16[16,48,256]{2,1,0:T(8,128)(2,1)}), bf16[16,48,256]{2,1,0:T(8,128)(2,1)S(1)}, u32[]{:S(2)}, u32[]{:S(2)}) async-start(bf16[16,48,256]{2,1,0:T(8,128)(2,1)} %bitcast.22), calls=%async_computation.6 | async-start | bytes 786432 | tf_op jit(solution)/shard_map/all_to_all | solution.py:139
  154.8 4.6 %copy-start.3 = (bf16[768,1792]{1,0:T(8,128)(2,1)S(1)}, bf16[768,1792]{1,0:T(8,128)(2,1)}, u32[]{:S(2)}) copy-start(bf16[768,1792]{1,0:T(8,128)(2,1)} %copy-done.2) | copy-start | bytes 8257540
  154.8 4.6 %copy-start.10 = (bf16[768,256]{1,0:T(8,128)(2,1)S(1)}, bf16[768,256]{1,0:T(8,128)(2,1)}, u32[]{:S(2)}) copy-start(bf16[768,256]{1,0:T(8,128)(2,1)} %slice.38) | copy-start | bytes 1179652
  (4 other events, 9.0 us)
